TPU v7x, 128 devices: a whole 4x4x4 slice. The times are simulated.
128 devices in a mesh: orb: 32 (over y, x, core), grid: 4 (over z).
Axes of the slice: x: 4, y: 4, z: 4, core: 2. Of those that a mesh axis runs over, the one named last changes fastest.
Arguments:
- orbitals: bfloat16 [1024, 40, 1600], P('orb', 'grid')
- box_offset: int32 [1024, 3], replicated, may hold values from 0 to 235, as said below
- partner_slot: int32 [32, 32, 4], P('orb'), may hold values from -1 to 31, as said below
- first_slot: int32 [32, 32, 4], P('orb'), may hold values from -1 to 31, as said below
Outputs:
- exchange_terms: float32 [1024, 40, 1600], P('orb', 'grid')
- gram: float32 [1024, 1024], replicated
Inputs may be any that keep to these rules, and one draw needn't show every extreme that they name: `box_offset`: entries lie within 20 of one another along each of the three dimensions, and both ends of that span are reached. `partner_slot`: -1 marks an empty slot; every owner o has all 4 slots toward owner (o + 1) mod 32 live; where o equals d the two orbitals of a slot differ. `first_slot`: -1 exactly where partner_slot is -1.
All inputs are finite; a program needn't handle non-finite values.
Results may differ from a plain program's by a relative error of at most 0.0045.
The roundings to bfloat16 on the way count: a program that leaves them out, or rounds other values in their place, can miss the bound.
Values may be sent and summed in bfloat16 or wider, within the bound.
A program may use at most 192 MiB of HBM per device.

v0:
```python
import math

import jax
import jax.numpy as jnp
from jax import lax
from jax.sharding import PartitionSpec as P


def tables(box_edge):
    wave_number = jnp.arange(box_edge, dtype=jnp.float32) + 1.0
    sine_table = jnp.sqrt(2.0 / (box_edge + 1.0)) * jnp.sin(
        math.pi * wave_number[:, None] * wave_number[None, :] / (box_edge + 1.0)
    )
    plane_table = (
        (sine_table[:, None, :, None] * sine_table[None, :, None, :])
        .reshape(box_edge * box_edge, box_edge * box_edge)
        .astype(jnp.bfloat16)
    )
    eigen_one = 2.0 - 2.0 * jnp.cos(math.pi * wave_number / (box_edge + 1.0))
    eigen_sum = eigen_one[:, None, None] + eigen_one[None, :, None] + eigen_one[None, None, :]
    green_table = (1.0 / eigen_sum).reshape(box_edge, box_edge * box_edge)
    return (sine_table, plane_table, green_table)


def moved(source, delta):
    box_edge = source.shape[0]
    cubic = source.reshape(box_edge, box_edge, box_edge)
    cells = jnp.arange(box_edge, dtype=jnp.int32)
    along_x = cells + delta[0]
    along_y = cells + delta[1]
    along_z = cells + delta[2]

    def within(where_to):
        return (where_to >= 0) & (where_to < box_edge)

    inside = (
        within(along_x)[:, None, None]
        & within(along_y)[None, :, None]
        & within(along_z)[None, None, :]
    )
    cubic = jnp.take(cubic, jnp.clip(along_x, 0, box_edge - 1), axis=0)
    cubic = jnp.take(cubic, jnp.clip(along_y, 0, box_edge - 1), axis=1)
    cubic = jnp.take(cubic, jnp.clip(along_z, 0, box_edge - 1), axis=2)
    return jnp.where(inside, cubic, jnp.zeros((), source.dtype)).reshape(
        box_edge, box_edge * box_edge
    )


def solve_block(phi_first, phi_second, shifts, all_tables):
    sine_table, plane_table, green_table = all_tables
    box_edge = phi_first.shape[1]
    shifted = jax.vmap(moved)(phi_second, shifts)
    density = phi_first.astype(jnp.float32) * shifted.astype(jnp.float32)
    forward = jnp.einsum(
        "kx,sxq->skq", sine_table, density, precision=lax.Precision.HIGHEST
    ).astype(jnp.bfloat16)
    block_rows = forward.shape[0] * forward.shape[1]
    coeffs = jnp.dot(
        forward.reshape(block_rows, -1), plane_table, preferred_element_type=jnp.float32
    ).reshape(forward.shape)
    scaled = (green_table * coeffs).astype(jnp.bfloat16)
    inverse = jnp.dot(
        scaled.reshape(block_rows, -1), plane_table, preferred_element_type=jnp.float32
    ).reshape(forward.shape)
    potential = jnp.einsum("kx,sxq->skq", sine_table, inverse, precision=lax.Precision.HIGHEST)
    energy = jnp.sum(density * potential, axis=(1, 2)) / (box_edge * box_edge * box_edge)
    own_term = potential * shifted.astype(jnp.float32)
    product = (potential * phi_first.astype(jnp.float32)).astype(jnp.bfloat16)
    return (own_term, product, energy)


def on_device(orbitals, box_offset, partner_slot, first_slot):
    orb_count = lax.axis_size("orb")
    grid_count = lax.axis_size("grid")
    orb_index = lax.axis_index("orb")
    grid_index = lax.axis_index("grid")
    orb_dev, slab_rows, box_area = orbitals.shape
    box_edge = slab_rows * grid_count
    orbital_total = orb_dev * orb_count
    quarter = partner_slot.shape[2] // grid_count
    slot_total = orb_count * quarter
    block_size = 16
    block_count = slot_total // block_size
    all_tables = tables(box_edge)
    asked, asker_first = (
        lax.all_to_all(partner_slot[0], "orb", split_axis=0, concat_axis=0, tiled=True),
        lax.all_to_all(first_slot[0], "orb", split_axis=0, concat_axis=0, tiled=True),
    )

    def my_part(table):
        return lax.dynamic_slice_in_dim(table, grid_index * quarter, quarter, 1).reshape(-1)

    second_local = my_part(partner_slot[0])
    first_local = my_part(first_slot[0])
    asked_local = my_part(asked)
    asker_local = my_part(asker_first)
    slot_owner = jnp.repeat(jnp.arange(orb_count, dtype=jnp.int32), quarter)
    own_full = lax.all_gather(orbitals, "grid", axis=1, tiled=True)
    picked = jnp.take(own_full, jnp.maximum(asked_local, 0), axis=0)
    picked = jnp.where((asked_local >= 0)[:, None, None], picked, jnp.zeros((), jnp.bfloat16))
    partners = lax.all_to_all(
        picked.reshape(orb_count, quarter, box_edge, box_area),
        "orb",
        split_axis=0,
        concat_axis=0,
        tiled=True,
    )
    alive_slots = second_local >= 0
    first_clip = jnp.maximum(first_local, 0)
    first_global = orb_index * orb_dev + first_clip
    second_global = slot_owner * orb_dev + jnp.maximum(second_local, 0)
    slot_delta = box_offset[first_global] - box_offset[second_global]
    orbital_ids = jnp.arange(orb_dev, dtype=jnp.int32)

    def blocked(values):
        return values.reshape((block_count, block_size) + values.shape[1:])

    def own_block(running, pieces):
        first_ids, partner_rows, shifts, alive = pieces
        phi_first = jnp.take(own_full, first_ids, axis=0)
        own_term, product, energy = solve_block(phi_first, partner_rows, shifts, all_tables)
        selector = ((first_ids[:, None] == orbital_ids[None, :]) & alive[:, None]).astype(
            jnp.float32
        )
        running = running + jnp.einsum(
            "sa,sxq->axq", selector, own_term, precision=lax.Precision.HIGHEST
        )
        return (running, (product, jnp.where(alive, energy, 0.0)))

    empty_terms = jnp.zeros((orb_dev, box_edge, box_area), jnp.float32)
    own_inputs = (
        blocked(first_clip),
        blocked(partners.reshape(slot_total, box_edge, box_area)),
        blocked(slot_delta),
        blocked(alive_slots),
    )
    terms_own, (products, energies) = lax.scan(own_block, empty_terms, own_inputs)
    energies = energies.reshape(-1)
    local_gram = (
        jnp.zeros((orbital_total, orbital_total), jnp.float32)
        .at[first_global, second_global]
        .add(energies)
    )
    gram = lax.psum(local_gram + local_gram.T, ("orb", "grid"))
    returned = lax.all_to_all(
        products.reshape(orb_count, quarter, box_edge, box_area),
        "orb",
        split_axis=0,
        concat_axis=0,
        tiled=True,
    )
    back_alive = asked_local >= 0
    back_second = jnp.maximum(asked_local, 0)
    back_first_global = slot_owner * orb_dev + jnp.maximum(asker_local, 0)
    back_delta = box_offset[back_first_global] - box_offset[orb_index * orb_dev + back_second]

    def back_block(running, pieces):
        second_ids, boxes, shifts, alive = pieces
        placed = jax.vmap(moved)(boxes, -shifts).astype(jnp.float32)
        selector = ((second_ids[:, None] == orbital_ids[None, :]) & alive[:, None]).astype(
            jnp.float32
        )
        return (
            running + jnp.einsum("sa,sxq->axq", selector, placed, precision=lax.Precision.HIGHEST),
            None,
        )

    back_inputs = (
        blocked(back_second),
        blocked(returned.reshape(slot_total, box_edge, box_area)),
        blocked(back_delta),
        blocked(back_alive),
    )
    terms_back, unused = lax.scan(back_block, empty_terms, back_inputs)
    exchange_terms = lax.psum_scatter(
        terms_own + terms_back, "grid", scatter_dimension=1, tiled=True
    )
    return (exchange_terms, gram)


def solution(mesh):
    placed = (P("orb", "grid", None), P(), P("orb", None, None), P("orb", None, None))
    return jax.shard_map(
        on_device,
        mesh=mesh,
        in_specs=placed,
        out_specs=(P("orb", "grid", None), P()),
        check_vma=False,
    )
```

profile of v0, /device:TPU:1, one launch (start us, length us, event | category | flops | bytes accessed | tf_op | source)
XLA Modules:
  0.0 912.0 jit_solution(7873641437081713540)
XLA Ops:
  27.7 34.2 %all-gather.2.cloned.1.call-done = bf16[32,40,1600]{2,0,1:T(8,128)(2,1)} async-done(((bf16[32,10,1600]{2,0,1:T(8,128)(2,1)}), bf16[32,40,1600]{2,0,1:T(8,128)(2,1)}) %all-gather.2.cloned.1.call-update) | async-done | bytes 4096016 | tf_op jit(solution)/shard_map/all_gather | solution.py:98
  91.2 45.0 %all-to-all-done.1 = bf16[32,1,40,1600]{3,2,1,0:T(8,128)(2,1)} async-done(((bf16[32,1,40,1600]{3,2,1,0:T(8,128)(2,1)}), bf16[32,1,40,1600]{3,2,1,0:T(8,128)(2,1)}, u32[]{:S(2)}, u32[]{:S(2)}) %all-to-all-start.1) | async-done | bytes 4096032 | tf_op jit(solution)/shard_map/all_to_all | solution.py:101
  144.1 390.4 %while.28 = (s32[]{:T(128)}, f32[32,40,1600]{2,0,1:T(8,128)}, bf16[2,16,40,1600]{3,2,1,0:T(8,128)(2,1)}, f32[2,16]{1,0:T(2,128)S(1)}, s32[2,16]{1,0:T(2,128)S(1)...) while((s32[]{:T(128)}, f32[32,40,1600]{2,0,1:T(8,128)}, ...), condition=%wide.region_2.6_spmd.clone.clone, body=%wide.region_0.5_spmd.clone.clone.sunk | while | flops 7961804288 | bytes 163017712 | solution.py:137
  153.7 12.4 %gather_fusion.3 = bf16[640,40,40]{2,1,0:T(8,128)(2,1)} fusion(bf16[16,40,40,40]{3,2,1,0:T(8,128)(2,1)} %reshape.791, s32[640]{0:T(1024)S(1)} %reshape.792), kind=kCustom, calls=%fused_computation.3.clone.clone.1 | custom fusion | bytes 4101120 | tf_op jit(solution)/shard_map/while/body/eval_jaxpr/vmap(jit(_take))/gather | solution.py:41
  172.8 12.4 %gather_fusion.4 = bf16[640,40,40]{2,1,0:T(8,128)(2,1)} fusion(bf16[16,40,40,40]{3,1,2,0:T(8,128)(2,1)} %copy_select_fusion.5, s32[640]{0:T(1024)S(1)} %reshape.793), kind=kCustom, calls=%fused_computation.4.clone.clone.1 | custom fusion | bytes 4101120 | tf_op jit(solution)/shard_map/while/body/eval_jaxpr/vmap(jit(_take))/gather | solution.py:42
  202.3 12.4 %gather_fusion.5 = bf16[640,40,40]{2,1,0:T(8,128)(2,1)} fusion(bf16[16,40,40,40]{2,1,3,0:T(8,128)(2,1)} %select_bitcast_fusion.5, s32[640]{0:T(1024)S(1)} %reshape.794), kind=kCustom, calls=%fused_computation.5.clone.clone.1 | custom fusion | bytes 4101120 | tf_op jit(solution)/shard_map/while/body/eval_jaxpr/vmap(jit(_take))/gather | solution.py:43
  234.1 13.6 %copy.188 = f32[16,40,40,40]{3,2,1,0:T(8,128)} copy(f32[16,40,40,40]{3,0,2,1:T(8,128)} %fusion.132) | data formatting | bytes 8192000 | tf_op jit(solution)/shard_map/while/body/eval_jaxpr/convert_element_type | solution.py:53
  267.3 20.4 %reshape.796 = bf16[1600,1600,1]{1,0,2:T(8,128)(2,1)} reshape(bf16[40,40,40,40]{3,2,1,0:T(8,128)(2,1)} %multiply_convert_fusion.3) | data formatting | bytes 10240000 | tf_op jit(solution)/shard_map/convert_element_type | solution.py:17
  297.0 15.4 %fusion.135 = f32[16,40,1600]{2,1,0:T(8,128)} fusion(bf16[1600,1600,1]{1,0,2:T(8,128)(2,1)} %reshape.796, bf16[16,40,1600]{2,1,0:T(8,128)(2,1)} %fusion.134, f32[40,1600]{1,0:T(8,128)S(1)} %mul.346), kind=kOutput, calls=%fused_computation.84.clone.1 | convolution fusion | flops 6555648000 | bytes 11520000 | tf_op jit(solution)/shard_map/while/body/eval_jaxpr/dot_general | solution.py:62
  346.7 12.4 %gather_fusion.3 = bf16[640,40,40]{2,1,0:T(8,128)(2,1)} fusion(bf16[16,40,40,40]{3,2,1,0:T(8,128)(2,1)} %reshape.791, s32[640]{0:T(1024)S(1)} %reshape.792), kind=kCustom, calls=%fused_computation.3.clone.clone.1 | custom fusion | bytes 4101120 | tf_op jit(solution)/shard_map/while/body/eval_jaxpr/vmap(jit(_take))/gather | solution.py:41
  365.9 12.4 %gather_fusion.4 = bf16[640,40,40]{2,1,0:T(8,128)(2,1)} fusion(bf16[16,40,40,40]{3,1,2,0:T(8,128)(2,1)} %copy_select_fusion.5, s32[640]{0:T(1024)S(1)} %reshape.793), kind=kCustom, calls=%fused_computation.4.clone.clone.1 | custom fusion | bytes 4101120 | tf_op jit(solution)/shard_map/while/body/eval_jaxpr/vmap(jit(_take))/gather | solution.py:42
  395.3 12.4 %gather_fusion.5 = bf16[640,40,40]{2,1,0:T(8,128)(2,1)} fusion(bf16[16,40,40,40]{2,1,3,0:T(8,128)(2,1)} %select_bitcast_fusion.5, s32[640]{0:T(1024)S(1)} %reshape.794), kind=kCustom, calls=%fused_computation.5.clone.clone.1 | custom fusion | bytes 4101120 | tf_op jit(solution)/shard_map/while/body/eval_jaxpr/vmap(jit(_take))/gather | solution.py:43
  426.9 13.6 %copy.188 = f32[16,40,40,40]{3,2,1,0:T(8,128)} copy(f32[16,40,40,40]{3,0,2,1:T(8,128)} %fusion.132) | data formatting | bytes 8192000 | tf_op jit(solution)/shard_map/while/body/eval_jaxpr/convert_element_type | solution.py:53
  460.0 20.5 %reshape.796 = bf16[1600,1600,1]{1,0,2:T(8,128)(2,1)} reshape(bf16[40,40,40,40]{3,2,1,0:T(8,128)(2,1)} %multiply_convert_fusion.3) | data formatting | bytes 10240000 | tf_op jit(solution)/shard_map/convert_element_type | solution.py:17
  489.8 15.4 %fusion.135 = f32[16,40,1600]{2,1,0:T(8,128)} fusion(bf16[1600,1600,1]{1,0,2:T(8,128)(2,1)} %reshape.796, bf16[16,40,1600]{2,1,0:T(8,128)(2,1)} %fusion.134, f32[40,1600]{1,0:T(8,128)S(1)} %mul.346), kind=kOutput, calls=%fused_computation.84.clone.1 | convolution fusion | flops 6555648000 | bytes 11520000 | tf_op jit(solution)/shard_map/while/body/eval_jaxpr/dot_general | solution.py:62
  564.8 29.3 %all-to-all-done.3 = bf16[32,1,40,1600]{3,2,1,0:T(8,128)(2,1)} async-done(((bf16[32,1,40,1600]{3,2,1,0:T(8,128)(2,1)}), bf16[32,1,40,1600]{3,2,1,0:T(8,128)(2,1)}, u32[]{:S(2)}, u32[]{:S(2)}) %all-to-all-start.3) | async-done | bytes 4096032 | tf_op jit(solution)/shard_map/all_to_all | solution.py:145
  594.1 213.6 %while.27 = (s32[]{:T(128)}, f32[32,40,1600]{2,0,1:T(8,128)}, s32[2,16]{1,0:T(2,128)S(1)}, pred[2,16]{1,0:T(4,128)(4,1)S(1)}, s32[2,16,3]{1,2,0:T(4,128)S(1)}, /...) while((s32[]{:T(128)}, f32[32,40,1600]{2,0,1:T(8,128)}, s32[2,16]{1,0:T(2,128)S(1)}, ...), condition=%wide.region_4.8_spmd.clone, body=%wide.region_3.7_spmd.clone.sunk | while | flops 74817712 | bytes 67685352 | solution.py:174
  603.8 12.4 %gather_fusion = bf16[640,40,40]{2,1,0:T(8,128)(2,1)} fusion(bf16[16,40,40,40]{3,2,1,0:T(8,128)(2,1)} %reshape.778, s32[640]{0:T(1024)S(1)} %reshape.779), kind=kCustom, calls=%fused_computation.clone.clone.1 | custom fusion | bytes 4101120 | tf_op jit(solution)/shard_map/while/body/eval_jaxpr/vmap(jit(_take))/gather | solution.py:41
  622.9 12.5 %gather_fusion.1 = bf16[640,40,40]{2,1,0:T(8,128)(2,1)} fusion(bf16[16,40,40,40]{3,1,2,0:T(8,128)(2,1)} %copy_select_fusion.4, s32[640]{0:T(1024)S(1)} %reshape.780), kind=kCustom, calls=%fused_computation.1.clone.clone.1 | custom fusion | bytes 4101120 | tf_op jit(solution)/shard_map/while/body/eval_jaxpr/vmap(jit(_take))/gather | solution.py:42
  652.4 12.3 %gather_fusion.2 = bf16[640,40,40]{2,1,0:T(8,128)(2,1)} fusion(bf16[16,40,40,40]{2,1,3,0:T(8,128)(2,1)} %select_bitcast_fusion.4, s32[640]{0:T(1024)S(1)} %reshape.781), kind=kCustom, calls=%fused_computation.2.clone.clone.1 | custom fusion | bytes 4101120 | tf_op jit(solution)/shard_map/while/body/eval_jaxpr/vmap(jit(_take))/gather | solution.py:43
  708.6 12.5 %gather_fusion = bf16[640,40,40]{2,1,0:T(8,128)(2,1)} fusion(bf16[16,40,40,40]{3,2,1,0:T(8,128)(2,1)} %reshape.778, s32[640]{0:T(1024)S(1)} %reshape.779), kind=kCustom, calls=%fused_computation.clone.clone.1 | custom fusion | bytes 4101120 | tf_op jit(solution)/shard_map/while/body/eval_jaxpr/vmap(jit(_take))/gather | solution.py:41
  728.0 12.5 %gather_fusion.1 = bf16[640,40,40]{2,1,0:T(8,128)(2,1)} fusion(bf16[16,40,40,40]{3,1,2,0:T(8,128)(2,1)} %copy_select_fusion.4, s32[640]{0:T(1024)S(1)} %reshape.780), kind=kCustom, calls=%fused_computation.1.clone.clone.1 | custom fusion | bytes 4101120 | tf_op jit(solution)/shard_map/while/body/eval_jaxpr/vmap(jit(_take))/gather | solution.py:42
  757.4 12.3 %gather_fusion.2 = bf16[640,40,40]{2,1,0:T(8,128)(2,1)} fusion(bf16[16,40,40,40]{2,1,3,0:T(8,128)(2,1)} %select_bitcast_fusion.4, s32[640]{0:T(1024)S(1)} %reshape.781), kind=kCustom, calls=%fused_computation.2.clone.clone.1 | custom fusion | bytes 4101120 | tf_op jit(solution)/shard_map/while/body/eval_jaxpr/vmap(jit(_take))/gather | solution.py:43
  817.9 82.3 %reduce-scatter.2.cloned.1.call-done = f32[32,10,1600]{2,0,1:T(8,128)} async-done(((f32[32,40,1600]{2,0,1:T(8,128)}), f32[32,10,1600]{2,0,1:T(8,128)}) %reduce-scatter.2.cloned.1.call-update) | async-done | bytes 2048016 | tf_op jit(solution)/shard_map/reduce_scatter | solution.py:175
  (201 shorter events, 454.2 us)
Async XLA Ops:
  7.2 54.8 %all-gather.2.cloned.1.call-start = ((), (), s32[]{:S(2)}) async-start(), calls=%async_computation.5 | async-start | bytes 5324800 | tf_op jit(solution)/shard_map/all_gather | solution.py:98
  9.3 15.5 %all-to-all-start = ((s32[32,1,4]{2,1,0:T(1,128)}), s32[32,1,4]{2,1,0:T(1,128)S(1)}, u32[]{:S(2)}, u32[]{:S(2)}) async-start(s32[32,1,4]{2,1,0:T(1,128)} %copy.136), calls=%async_computation | async-start | bytes 32768 | tf_op jit(solution)/shard_map/all_to_all | solution.py:86
  26.0 46.7 %copy-start.7 = (pred[32]{0:T(512)(128)(4,1)}, pred[32]{0:T(512)(128)(4,1)S(1)}, u32[]{:S(2)}) copy-start(pred[32]{0:T(512)(128)(4,1)S(1)} %get-tuple-element.433) | copy-start | bytes 100
  27.7 39.7 %copy-start.9 = (s32[32]{0:T(128)}, s32[32]{0:T(128)S(1)}, u32[]{:S(2)}) copy-start(s32[32]{0:T(128)S(1)} %get-tuple-element.356) | copy-start | bytes 388
  77.6 7.8 copy-start.6
  77.6 7.9 copy-start.5
  77.6 8.0 copy-start.4
  77.6 58.6 %all-to-all-start.1 = ((bf16[32,1,40,1600]{3,2,1,0:T(8,128)(2,1)}), bf16[32,1,40,1600]{3,2,1,0:T(8,128)(2,1)}, u32[]{:S(2)}, u32[]{:S(2)}) async-start(bf16[32,1,40,1600]{3,2,1,0:T(8,128)(2,1)} %fusion.84), calls=%async_computation.1 | async-start | bytes 8519680 | tf_op jit(solution)/shard_map/all_to_all | solution.py:101
  85.8 58.3 %copy-start.1 = (s32[1024,3]{1,0:T(8,128)}, s32[1024,3]{1,0:T(8,128)S(1)}, u32[]{:S(2)}) copy-start(s32[1024,3]{1,0:T(8,128)S(1)} %copy.133) | copy-start | bytes 36868
  136.2 398.2 %all-to-all-start.2 = ((s32[32,1,4]{2,1,0:T(1,128)}), s32[32,1,4]{2,1,0:T(1,128)}, u32[]{:S(2)}, u32[]{:S(2)}) async-start(s32[32,1,4]{2,1,0:T(1,128)} %copy.141), calls=%async_computation.2 | async-start | bytes 32768 | tf_op jit(solution)/shard_map/all_to_all | solution.py:87
  324.1 10.8 %copy-start = (f32[16,1600,40]{1,2,0:T(8,128)S(1)}, f32[16,1600,40]{1,2,0:T(8,128)}, u32[]{:S(2)}) copy-start(f32[16,1600,40]{1,2,0:T(8,128)} %get-tuple-element.610) | copy-start | bytes 12288004 | tf_op jit(solution)/shard_map/while
  517.1 12.1 %copy-start = (f32[16,1600,40]{1,2,0:T(8,128)S(1)}, f32[16,1600,40]{1,2,0:T(8,128)}, u32[]{:S(2)}) copy-start(f32[16,1600,40]{1,2,0:T(8,128)} %get-tuple-element.610) | copy-start | bytes 12288004 | tf_op jit(solution)/shard_map/while
  534.5 7.8 copy-start.10
  534.5 7.9 copy-start.8
  534.5 9.4 %copy-start.2 = (s32[1024,3]{1,0:T(8,128)S(1)}, s32[1024,3]{1,0:T(8,128)}, u32[]{:S(2)}) copy-start(s32[1024,3]{1,0:T(8,128)} %copy-done.1) | copy-start | bytes 36868
  534.5 10.0 %copy-start.11 = (s32[32]{0:T(128)S(1)}, s32[32]{0:T(128)}, u32[]{:S(2)}) copy-start(s32[32]{0:T(128)} %get-tuple-element.355) | copy-start | bytes 388
  534.5 59.6 %all-to-all-start.3 = ((bf16[32,1,40,1600]{3,2,1,0:T(8,128)(2,1)}), bf16[32,1,40,1600]{3,2,1,0:T(8,128)(2,1)}, u32[]{:S(2)}, u32[]{:S(2)}) async-start(bf16[32,1,40,1600]{3,2,1,0:T(8,128)(2,1)} %bitcast.234), calls=%async_computation.3 | async-start | bytes 8519680 | tf_op jit(solution)/shard_map/all_to_all | solution.py:145
  542.2 5.6 copy-start.3
  542.2 275.7 %all-reduce.2.cloned.1.call-start = ((), (), s32[]{:S(2)}) async-start(), calls=%async_computation.7 | async-start | bytes 8388608 | tf_op jit(solution)/shard_map/psum | solution.py:144
  564.8 335.5 %reduce-scatter.2.cloned.1.call-start = ((), (), s32[]{:S(2)}) async-start(), calls=%async_computation.6 | async-start | bytes 10649600 | tf_op jit(solution)/shard_map/reduce_scatter | solution.py:175
Sparse Core Ops, SparseCore 0:
  9.7 52.2 all-gather.1
  564.9 166.7 all-reduce.1
  818.0 82.1 reduce-scatter.1
where the time goes:
time: 922 us; the launch traced here: 912 us
  local copies, waits for them, and re-layouts  423 us (46%)
  waiting for transfers between devices  198 us (21%)
  other arithmetic  134 us (15%)
  matrix products  106 us (11%)
  starting transfers between devices  32 us (3%)
  between operations  14.4 us (2%)
    gather x12, local copies, waits for them, and re-layouts, moved(): cubic = jnp.take(cubic, jnp.clip(along_z, 0, box_edge - 1), axis=2)  93.9 us
    gather x12, local copies, waits for them, and re-layouts, moved(): cubic = jnp.take(cubic, jnp.clip(along_y, 0, box_edge - 1), axis=1)  92.8 us
    reduce_scatter x1, waiting for transfers between devices, on_device(): lax.psum_scatter(terms_own + terms_back, 'grid', scatter_dimension=1, til...  82.3 us
    gather x8, local copies, waits for them, and re-layouts, moved(): cubic = jnp.take(cubic, jnp.clip(along_x, 0, box_edge - 1), axis=0)  50 us
    convert_element_type x4, local copies, waits for them, and re-layouts, solve_block(): density = phi_first.astype(jnp.float32) * shifted.astype(jnp.float32)  47.8 us
    all_to_all x1, waiting for transfers between devices, on_device(): lax.all_to_all(picked.reshape(orb_count, quarter, box_edge, box_area), 'o...  45 us
    convert_element_type x2, local copies, waits for them, and re-layouts, tables(): plane_table = (sine_table[:, None, :, None] * sine_table[None, :, None, :...  40.9 us
    all_gather x1, waiting for transfers between devices, on_device(): own_full = lax.all_gather(orbitals, 'grid', axis=1, tiled=True)  34.2 us
  transfers between devices with their start and end apart: 7, of which 5 were waited for; matrix products, arithmetic and copies ran while one was open for 70% of the time, Pallas kernels for 0%

commit v1 on v0

v1 whole, which is shorter than its diff:
```python
import functools
import math

import jax
import jax.numpy as jnp
import ml_dtypes
import numpy as np
from jax import lax
from jax.experimental import pallas as pl
from jax.experimental.pallas import tpu as pltpu
from jax.sharding import PartitionSpec as P

BF16 = jnp.bfloat16
F32 = jnp.float32
VMEM = pl.BlockSpec(memory_space=pltpu.VMEM)
SMEM = pl.BlockSpec(memory_space=pltpu.SMEM)
EDGE = 40
AREA = 1600
ORB_DEV = 32
CAP = 4
SLOTS = 32
BATCH = 8
PADDED = 1792
TOP = 24
LEFT = 896
TILES = [(at, min(128, AREA - at)) for at in range(0, AREA, 128)]
WIDE = [(at, min(256, AREA - at)) for at in range(0, AREA, 256)]


@functools.cache
def tables():
    number = np.arange(EDGE, dtype=np.float64) + 1.0
    sine = np.sqrt(2.0 / (EDGE + 1.0)) * np.sin(
        math.pi * number[:, None] * number[None, :] / (EDGE + 1.0)
    )
    sine32 = sine.astype(np.float32)
    plane = (sine32[:, None, :, None] * sine32[None, :, None, :]).reshape(AREA, AREA)
    plane = np.pad(plane, ((0, 0), (0, PADDED - AREA))).astype(ml_dtypes.bfloat16)
    eigen = 2.0 - 2.0 * np.cos(math.pi * number / (EDGE + 1.0))
    green = 1.0 / (eigen[:, None, None] + eigen[None, :, None] + eigen[None, None, :])
    green = np.pad(green.reshape(EDGE, AREA), ((0, 0), (0, PADDED - AREA)))
    green = np.tile(green.astype(np.float32), (2, 1))
    high = sine32.astype(ml_dtypes.bfloat16)
    low = (sine32 - high.astype(np.float32)).astype(ml_dtypes.bfloat16)
    two = np.eye(2, dtype=np.float32)
    pair_high = np.kron(two, high.astype(np.float32))
    pair_low = np.kron(two, low.astype(np.float32))
    sine_pair = np.concatenate([pair_high, pair_high, pair_low], 1).astype(ml_dtypes.bfloat16)
    along_z = np.tile(np.arange(1664, dtype=np.int32) % EDGE, (8, 1))
    return sine_pair, plane, green, along_z


def selector(index_of):
    column = lax.broadcasted_iota(jnp.int32, (8, 256), 1)
    row = lax.broadcasted_iota(jnp.int32, (8, 256), 0)
    offset = column - row * ORB_DEV
    blocks = []
    for slot in range(SLOTS):
        index = index_of(slot)
        index = jnp.where(index < 0, 100000, index)
        blocks.append((offset == index).astype(F32))
    return jnp.concatenate(blocks, 0)


def pick_kernel(place, partner, first, own, picked, phi):
    me, level = place[0], place[1]
    sel_picked = selector(lambda s: partner[s * 128 + me * CAP + level]).astype(BF16)
    sel_phi = selector(lambda s: first[me * 128 + s * CAP + level]).astype(BF16)
    both = jnp.concatenate([sel_picked, sel_phi], 0)
    for at, width in WIDE:
        cols = slice(at, at + width)
        for start in range(0, EDGE, 16):
            parts = []
            for chunk in range(start, min(start + 16, EDGE), 8):
                source = own[chunk : chunk + 8, :, cols].reshape(256, width)
                out = jnp.dot(both, source, preferred_element_type=F32)
                parts.append(out.reshape(2 * SLOTS, 8, width))
            out = jnp.concatenate(parts, 1).astype(BF16)
            rows = slice(start, start + out.shape[1])
            picked[:, rows, cols] = out[:SLOTS]
            phi[:, rows, cols] = out[SLOTS:]


def shift_tiles(pad, along_z, deltas, emit):
    dx, dy, dz = deltas
    start = LEFT + EDGE * dy + dz
    whole = lax.div(start, 128)
    part = start - whole * 128
    turn = lax.rem(128 - part, 128)
    lane = lax.broadcasted_iota(jnp.int32, (EDGE, 128), 1)
    from_here = lane < 128 - part
    rows = pl.ds(TOP + dx, EDGE)

    def turned(tile):
        return pltpu.roll(pad[whole + tile, rows, :], turn, 1)

    here = turned(0)
    for tile, (at, width) in enumerate(TILES):
        after = turned(tile + 1)
        out = jnp.where(from_here, here, after)
        z = along_z[:, at : at + 128] + dz
        inside = (z >= 0) & (z < EDGE)
        out = jnp.where(inside[None], out.reshape(EDGE // 8, 8, 128), 0.0).reshape(EDGE, 128)
        emit(at, width, out)
        here = after


def solve_kernel(
    place, partner, first, offset, partners, phis, sine_pair, plane, green, along_z,
    returned, own_terms, energies,
    live, pad, den, stack, forward, scaled, inverse, shifted, potential,
):
    me, level = place[0], place[1]

    def compact(slot, count):
        alive = partner[me * 128 + slot * CAP + level] >= 0
        energies[slot] = 0.0

        @pl.when(alive)
        def _():
            live[count] = slot

        @pl.when(jnp.logical_not(alive))
        def _():
            returned[slot] = jnp.zeros((EDGE, AREA), BF16)
            own_terms[slot] = jnp.zeros((EDGE, AREA), BF16)

        return count + alive.astype(jnp.int32)

    count = lax.fori_loop(0, SLOTS, compact, jnp.int32(0))
    pad[...] = jnp.zeros_like(pad)
    den[...] = jnp.zeros_like(den)

    def deltas_of(slot):
        at = me * 128 + slot * CAP + level
        i = (me * ORB_DEV + first[at]) * 3
        j = (slot * ORB_DEV + partner[at]) * 3
        return tuple(offset[i + axis] - offset[j + axis] for axis in range(3))

    def split(value):
        high = value.astype(BF16)
        return high, (value - high.astype(F32)).astype(BF16)

    def sine_product(cols):
        return jnp.dot(sine_pair[...], stack[:, cols], preferred_element_type=F32)

    def batch(index, _):
        base = index * BATCH
        pairs = lax.div(jnp.minimum(count - base, BATCH) + 1, 2)

        def before(pair, _):
            for side in range(2):
                position = base + pair * 2 + side
                rows = pl.ds(pl.multiple_of(pair * 80 + side * EDGE, 8), EDGE)

                @pl.when(position < count)
                def _():
                    slot = live[position]
                    for at, width in TILES:
                        pad[(LEFT + at) // 128, TOP : TOP + EDGE, :width] = partners[
                            slot, :, at : at + width
                        ].astype(F32)

                    def emit(at, width, out):
                        shifted[rows, at : at + 128] = out
                        phi = phis[slot, :, at : at + width].astype(F32)
                        den[side * EDGE : (side + 1) * EDGE, at : at + width] = (
                            phi * out[:, :width]
                        )

                    shift_tiles(pad, along_z, deltas_of(slot), emit)

            for at, width in TILES:
                cols = slice(at, at + width)
                high, low = split(den[:, cols])
                stack[0:80, cols] = high
                stack[80:160, cols] = low
                stack[160:240, cols] = high
            rows = pl.ds(pl.multiple_of(pair * 80, 16), 80)
            for at, width in WIDE:
                cols = slice(at, at + width)
                forward[rows, cols] = sine_product(cols).astype(BF16)
            return 0

        lax.fori_loop(0, pairs, before, 0)

        def to_coeffs(step, _):
            cols = pl.ds(pl.multiple_of(step * 256, 256), 256)
            coeffs = jnp.dot(forward[...], plane[:, cols], preferred_element_type=F32)
            for pair in range(BATCH // 2):
                scaled[pair * 80 : pair * 80 + 80, cols] = (
                    green[:, cols] * coeffs[pair * 80 : pair * 80 + 80]
                ).astype(BF16)
            return 0

        lax.fori_loop(0, PADDED // 256, to_coeffs, 0)

        def to_inverse(step, _):
            cols = pl.ds(pl.multiple_of(step * 256, 256), 256)
            inverse[:, cols] = jnp.dot(
                scaled[:, :AREA], plane[:, cols], preferred_element_type=F32
            )
            return 0

        lax.fori_loop(0, PADDED // 256, to_inverse, 0)

        def after(pair, _):
            rows = pl.ds(pl.multiple_of(pair * 80, 16), 80)
            for at, width in TILES:
                cols = slice(at, at + width)
                high, low = split(inverse[rows, cols])
                stack[0:80, cols] = high
                stack[80:160, cols] = low
                stack[160:240, cols] = high
            for at, width in WIDE:
                cols = slice(at, at + width)
                potential[:, cols] = sine_product(cols)
            for side in range(2):
                position = base + pair * 2 + side
                half = pl.ds(pl.multiple_of(pair * 80 + side * EDGE, 8), EDGE)

                @pl.when(position < count)
                def _():
                    slot = live[position]
                    energy = jnp.zeros((EDGE, 128), F32)
                    for at, width in TILES:
                        cols = slice(at, at + width)
                        phi = phis[slot, :, cols].astype(F32)
                        solved = potential[side * EDGE : (side + 1) * EDGE, cols]
                        term = solved * shifted[half, cols]
                        own_terms[slot, :, cols] = term.astype(BF16)
                        cell = term * phi
                        if width < 128:
                            cell = jnp.concatenate(
                                [cell, jnp.zeros((EDGE, 128 - width), F32)], 1
                            )
                        energy = energy + cell
                        pad[(LEFT + at) // 128, TOP : TOP + EDGE, :width] = (
                            (solved * phi).astype(BF16).astype(F32)
                        )
                    energies[slot] = jnp.sum(energy) / (EDGE * EDGE * EDGE)

                    back = tuple(-delta for delta in deltas_of(slot))

                    def emit(at, width, out):
                        returned[slot, :, at : at + width] = out[:, :width].astype(BF16)

                    shift_tiles(pad, along_z, back, emit)

            return 0

        lax.fori_loop(0, pairs, after, 0)
        return 0

    lax.fori_loop(0, lax.div(count + BATCH - 1, BATCH), batch, 0)


def sum_kernel(place, partner, first, returned, own_terms, total):
    me, level = place[0], place[1]
    back = selector(lambda s: partner[s * 128 + me * CAP + level]).T.astype(BF16)
    ahead = selector(lambda s: first[me * 128 + s * CAP + level]).T.astype(BF16)
    for at, width in WIDE:
        cols = slice(at, at + width)
        for start in range(0, EDGE, 16):
            stop = min(start + 16, EDGE)
            boxes = returned[:, start:stop, cols].astype(F32)
            terms = own_terms[:, start:stop, cols].astype(F32)
            for chunk in range(start, stop, 8):
                part = slice(chunk - start, chunk - start + 8)
                out = jnp.dot(
                    back,
                    boxes[:, part].reshape(256, width).astype(BF16),
                    preferred_element_type=F32,
                ) + jnp.dot(
                    ahead,
                    terms[:, part].reshape(256, width).astype(BF16),
                    preferred_element_type=F32,
                )
                total[chunk : chunk + 8, :, cols] = out.reshape(8, ORB_DEV, width).astype(
                    BF16
                )


def gram_kernel(partner, first, energy, gram, half):
    orbitals = gram.shape[0]
    row = lax.broadcasted_iota(jnp.int32, (orbitals, 128), 0)
    slot = lax.broadcasted_iota(jnp.int32, (orbitals, 128), 1)
    owner_here = lax.div(row, ORB_DEV) == lax.div(slot, CAP)
    within = lax.rem(row, ORB_DEV)
    first_row = lax.broadcasted_iota(jnp.int32, (ORB_DEV, 128), 0)

    def owner(index, _):
        here = pl.ds(index, 1)
        second = (owner_here & (within == partner[here, :])).astype(F32).astype(BF16)
        value = jnp.where(first_row == first[here, :], energy[here, :], 0.0)
        high = value.astype(BF16)
        rest = value - high.astype(F32)
        middle = rest.astype(BF16)
        low = (rest - middle.astype(F32)).astype(BF16)
        parts = jnp.concatenate([high, middle, low], 0)
        out = lax.dot_general(
            parts, second, (((1,), (1,)), ((), ())), preferred_element_type=F32
        )
        rows = pl.ds(pl.multiple_of(index * ORB_DEV, ORB_DEV), ORB_DEV)
        half[rows, :] = out[0:32] + out[32:64] + out[64:96]
        return 0

    lax.fori_loop(0, orbitals // ORB_DEV, owner, 0)
    for y in range(0, orbitals, 128):
        for x in range(0, orbitals, 128):
            gram[y : y + 128, x : x + 128] = (
                half[y : y + 128, x : x + 128] + half[x : x + 128, y : y + 128].T
            )


def params(mebibytes, **more):
    return pltpu.CompilerParams(vmem_limit_bytes=mebibytes * 2**20, **more)


BOXES = jax.ShapeDtypeStruct((SLOTS, EDGE, AREA), BF16)


def pick(place, partner, first, own):
    return pl.pallas_call(
        pick_kernel,
        out_shape=(BOXES, BOXES),
        in_specs=[SMEM, SMEM, SMEM, VMEM],
        out_specs=(VMEM, VMEM),
        compiler_params=params(48),
        name="pick",
    )(place, partner, first, own)


def solve(place, partner, first, offset, partners, phis):
    constants = [jnp.asarray(table) for table in tables()]
    return pl.pallas_call(
        solve_kernel,
        out_shape=(BOXES, BOXES, jax.ShapeDtypeStruct((SLOTS,), F32)),
        in_specs=[SMEM] * 4 + [VMEM] * 6,
        out_specs=(VMEM, VMEM, SMEM),
        scratch_shapes=[
            pltpu.SMEM((SLOTS + 8,), jnp.int32),
            pltpu.VMEM((27, 88, 128), F32),
            pltpu.VMEM((80, 1664), F32),
            pltpu.VMEM((240, AREA), BF16),
            pltpu.VMEM((BATCH * EDGE, AREA), BF16),
            pltpu.VMEM((BATCH * EDGE, PADDED), BF16),
            pltpu.VMEM((BATCH * EDGE, PADDED), F32),
            pltpu.VMEM((BATCH * EDGE, 1664), F32),
            pltpu.VMEM((80, AREA), F32),
        ],
        compiler_params=params(58),
        name="solve",
    )(place, partner, first, offset, partners, phis, *constants)


def sum_terms(place, partner, first, returned, own_terms):
    return pl.pallas_call(
        sum_kernel,
        out_shape=jax.ShapeDtypeStruct((EDGE, ORB_DEV, AREA), BF16),
        in_specs=[SMEM] * 3 + [VMEM] * 2,
        out_specs=VMEM,
        compiler_params=params(48),
        name="sum_terms",
    )(place, partner, first, returned, own_terms)


def gram_of(partner, first, energy, orbitals):
    return pl.pallas_call(
        gram_kernel,
        out_shape=jax.ShapeDtypeStruct((orbitals, orbitals), F32),
        in_specs=[VMEM] * 3,
        out_specs=VMEM,
        scratch_shapes=[pltpu.VMEM((orbitals, orbitals), F32)],
        compiler_params=params(32),
        name="gram",
    )(partner, first, energy)


def on_device(orbitals, box_offset, partner_slot, first_slot):
    orb_count = lax.axis_size("orb")
    place = jnp.stack([lax.axis_index("orb"), lax.axis_index("grid")]).astype(jnp.int32)
    own = lax.all_gather(orbitals.transpose(1, 0, 2), "grid", axis=0, tiled=True)
    lists = lax.all_gather(
        jnp.concatenate([partner_slot, first_slot], 0).reshape(1, 2, -1), "orb", tiled=True
    )
    partner_rows, first_rows = lists[:, 0], lists[:, 1]
    partner, first = partner_rows.reshape(-1), first_rows.reshape(-1)
    picked, phis = pick(place, partner, first, own)
    partners = lax.all_to_all(picked, "orb", split_axis=0, concat_axis=0, tiled=True)
    products, own_terms, energies = solve(
        place, partner, first, box_offset.reshape(-1), partners, phis
    )
    returned = lax.all_to_all(products, "orb", split_axis=0, concat_axis=0, tiled=True)
    shared = lax.all_gather(energies, ("orb", "grid"))
    shared = shared.reshape(orb_count, CAP, orb_count).transpose(0, 2, 1)
    gram = gram_of(
        partner_rows, first_rows, shared.reshape(orb_count, -1), orb_count * ORB_DEV
    )
    total = sum_terms(place, partner, first, returned, own_terms)
    terms = lax.psum_scatter(total, "grid", scatter_dimension=0, tiled=True)
    return (terms.astype(F32).transpose(1, 0, 2), gram)


def solution(mesh):
    placed = (P("orb", "grid", None), P(), P("orb", None, None), P("orb", None, None))
    return jax.shard_map(
        on_device,
        mesh=mesh,
        in_specs=placed,
        out_specs=(P("orb", "grid", None), P()),
        check_vma=False,
    )
```

time: 922 us -> 326 us (0.35); the launches traced: 912 us -> 326 us
  local copies, waits for them, and re-layouts: 423 us -> 6.41 us
  blocking collectives: 0 us -> 160 us
  other arithmetic: 134 us -> 3.51 us
  waiting for transfers between devices: 198 us -> 77.7 us
  matrix products: 106 us -> 0 us
  Pallas kernels: 0 us -> 56 us
  starting transfers between devices: 32 us -> 7.67 us
    gather x39 -> x0, local copies, waits for them, and re-layouts: 250 us -> none  [the longest x12 93.9 us: moved(): cubic = jnp.take(cubic, jnp.clip(along_z, 0, box_edge - 1), axis=2)]
    dot_general x10 -> x0, matrix products: 106 us -> none  [the longest x2 30.9 us: solve_block(): jnp.dot(scaled.reshape(block_rows, -1), plane_table, preferred_element_ty...]
    convert_element_type x6 -> x0, local copies, waits for them, and re-layouts: 88.7 us -> none  [the longest x4 47.8 us: solve_block(): density = phi_first.astype(jnp.float32) * shifted.astype(jnp.float32)]
    reduce_scatter x1, waiting for transfers between devices: 82.3 us -> 0.01 us  [on_device(): terms = lax.psum_scatter(total, 'grid', scatter_dimension=0, tiled=True)]
    select_n x17 -> x0, other arithmetic: 68.5 us -> none  [the longest x4 26.1 us: moved(): cubic = jnp.take(cubic, jnp.clip(along_x, 0, box_edge - 1), axis=0)]
    unnamed x0 -> x1, blocking collectives: none -> 68.1 us
    all_to_all x0 -> x1, blocking collectives: none -> 66.4 us  [on_device(): lax.all_to_all(products, 'orb', split_axis=0, concat_axis=0, tiled=True)]
    pallas_call x0 -> x4, Pallas kernels: none -> 56 us  [the longest x1 32.5 us: solve(): pl.pallas_call(solve_kernel, out_shape=(BOXES, BOXES, jax.ShapeDtypeStruc...]
  transfers between devices with their start and end apart: 7 -> 3, of which waited for: 5 -> 2; matrix products, arithmetic and copies ran while one was open for 70% -> 1% of each run, Pallas kernels for 0% -> 3%
where the time goes in v1:
time: 326 us
  blocking collectives  160 us (49%)
  waiting for transfers between devices  77.7 us (24%)
  Pallas kernels  56 us (17%)
  between operations  14.2 us (4%)
  starting transfers between devices  7.67 us (2%)
  local copies, waits for them, and re-layouts  6.41 us (2%)
  other arithmetic  3.51 us (1%)
    unnamed x1, blocking collectives  68.1 us
    all_to_all x1, blocking collectives, on_device(): lax.all_to_all(products, 'orb', split_axis=0, concat_axis=0, tiled=True)  66.4 us
    all_to_all x1, waiting for transfers between devices, on_device(): lax.all_to_all(picked, 'orb', split_axis=0, concat_axis=0, tiled=True)  49.7 us
    pallas_call x1, Pallas kernels, solve(): pl.pallas_call(solve_kernel, out_shape=(BOXES, BOXES, jax.ShapeDtypeStruc...  32.5 us
    all_gather x1, waiting for transfers between devices, on_device(): lax.all_gather(orbitals.transpose(1, 0, 2), 'grid', axis=0, tiled=True)  27.2 us
    all_gather x1, blocking collectives, on_device(): lax.all_gather(jnp.concatenate([partner_slot, first_slot], 0).reshape(1,...  25.8 us
    pallas_call x1, Pallas kernels, gram_of(): pl.pallas_call(gram_kernel, out_shape=jax.ShapeDtypeStruct((orbitals, orb...  10.6 us
    all_to_all x1, starting transfers between devices, on_device(): lax.all_to_all(picked, 'orb', split_axis=0, concat_axis=0, tiled=True)  7.59 us
  transfers between devices with their start and end apart: 3, of which 2 were waited for; matrix products, arithmetic and copies ran while one was open for 1% of the time, Pallas kernels for 3%

profile of v1, /device:TPU:1, one launch (start us, length us, event | category | flops | bytes accessed | tf_op | source)
XLA Modules:
  0.0 325.6 jit_solution(6549411666648840596)
XLA Ops:
  7.2 0.7 all-gather.3.cloned.1.call-update
  7.9 0.7 pad_add_fusion
  8.6 0.1 copy.16
  8.7 0.1 reshape.16
  8.8 25.8 %all_gather.12 = s32[32,2,128]{2,1,0:T(2,128)S(1)} all-gather(s32[1,2,128]{2,1,0:T(2,128)S(1)} %reshape.16), channel_id=1, replica_groups=mesh['orb'=32,'grid'=4] {'orb'}, dimensions={0}, use_global_device_ids=true | all-gather | bytes 33792 | tf_op jit(solution)/shard_map/all_gather | solution.py:384
  34.6 0.1 pad_add_fusion.1.place
  34.7 27.2 %all-gather.3.cloned.1.call-done.own = bf16[40,32,1600]{2,1,0:T(8,128)(2,1)} async-done(((bf16[10,32,1600]{2,1,0:T(8,128)(2,1)}), bf16[40,32,1600]{2,1,0:T(8,128)(2,1)}) %all-gather.3.cloned.1.call-update) | async-done | bytes 4096016 | tf_op jit(solution)/shard_map/all_gather | solution.py:383
  61.9 6.8 %pick.1 = (bf16[32,40,1600]{2,1,0:T(8,128)(2,1)S(1)}, bf16[32,40,1600]{2,1,0:T(8,128)(2,1)}) custom-call(s32[2]{0:T(128)S(1)} %pad_add_fusion.1.place, s32[4096]{0:T(1024)S(1)} %bitcast.21, s32[4096]{0:T(1024)S(1)} %bitcast.17, bf16[40,32,1600]{2,1,0:T(8,128)(2,1)} %all-gather.3.cloned.1.call-done.own), custom_call_target="tpu_custom_call" | custom-call | tf_op jit(solution)/shard_map/pick/pallas_call | solution.py:324
  68.7 2.0 copy-done.1
  70.7 7.6 %all-to-all-start = ((bf16[32,40,1600]{2,1,0:T(8,128)(2,1)}), bf16[32,40,1600]{2,1,0:T(8,128)(2,1)}, u32[]{:S(2)}, u32[]{:S(2)}) async-start(bf16[32,40,1600]{2,1,0:T(8,128)(2,1)} %copy-done.1), calls=%async_computation | async-start | bytes 8519680 | tf_op jit(solution)/shard_map/all_to_all | solution.py:390
  78.4 0.2 copy.19
  78.6 0.9 reshape.17.offset
  79.5 49.7 %all-to-all-done.partners = bf16[32,40,1600]{2,1,0:T(8,128)(2,1)} async-done(((bf16[32,40,1600]{2,1,0:T(8,128)(2,1)}), bf16[32,40,1600]{2,1,0:T(8,128)(2,1)}, u32[]{:S(2)}, u32[]{:S(2)}) %all-to-all-start) | async-done | bytes 4096032 | tf_op jit(solution)/shard_map/all_to_all | solution.py:390
  129.2 32.5 %solve.1 = (bf16[32,40,1600]{2,1,0:T(8,128)(2,1)}, bf16[32,40,1600]{2,1,0:T(8,128)(2,1)}, f32[32]{0:T(128)}) custom-call(s32[2]{0:T(128)} %copy-done.6, s32[4096]{0:T(1024)} %bitcast.22, s32[4096]{0:T(1024)} %bitcast.18, s32[3072]{0:T(1024)} %reshape.17.offset, bf16[32,40,1600]{2,1,0:T(8,128)(2,1)} %all-to-all-done.partners, ...), custom_call_target="tpu_custom_call" | custom-call | tf_op jit(solution)/shard_map/solve/pallas_call | solution.py:336
  161.7 66.4 %all_to_all.10.returned = bf16[32,40,1600]{2,1,0:T(8,128)(2,1)} all-to-all(bf16[32,40,1600]{2,1,0:T(8,128)(2,1)} %get-tuple-element.9), channel_id=1, replica_groups=mesh['orb'=32,'grid'=4] {'orb'}, dimensions={0} | all-to-all | bytes 8192000 | tf_op jit(solution)/shard_map/all_to_all | solution.py:394
  228.1 6.1 %sum_terms.1 = bf16[40,32,1600]{2,1,0:T(8,128)(2,1)S(1)} custom-call(s32[2]{0:T(128)S(1)} %copy-done.7, s32[4096]{0:T(1024)S(1)} %bitcast.23, s32[4096]{0:T(1024)S(1)} %bitcast.19, bf16[32,40,1600]{2,1,0:T(8,128)(2,1)} %all_to_all.10.returned, bf16[32,40,1600]{2,1,0:T(8,128)(2,1)} %get-tuple-element.10.own_terms), custom_call_target="tpu_custom_call" | custom-call | tf_op jit(solution)/shard_map/sum_terms/pallas_call | solution.py:358
  234.3 2.0 copy-done
  236.3 0.6 copy-done.9
  236.9 0.2 dynamic-update-slice
  237.1 68.1 %all-reduce = f32[4096]{0:T(1024)S(1)} all-reduce(f32[4096]{0:T(1024)S(1)} %dynamic-update-slice), channel_id=2, replica_groups=mesh['orb'=32,'grid'=4] {'orb','grid'}, use_global_device_ids=true, to_apply=%add | all-reduce | flops 4096 | bytes 32768
  305.2 0.1 reshape.18
  305.3 0.1 copy.20
  305.4 10.6 %gram.1 = f32[1024,1024]{1,0:T(8,128)} custom-call(s32[32,128]{1,0:T(8,128)S(1)} %bitcast.24, s32[32,128]{1,0:T(8,128)S(1)} %bitcast.20, f32[32,128]{1,0:T(8,128)S(1)} %copy.21.energy), custom_call_target="tpu_custom_call" | custom-call | tf_op jit(solution)/shard_map/gram/pallas_call | solution.py:369
  316.1 2.7 convert_bitcast_fusion
  (24 shorter events, 0.2 us)
Async XLA Ops:
  7.2 54.8 %all-gather.3.cloned.1.call-start = ((), (), s32[]{:S(2)}) async-start(), calls=%async_computation.3 | async-start | bytes 5324800 | tf_op jit(solution)/shard_map/all_gather | solution.py:383
  34.7 36.0 %copy-start.6 = (s32[2]{0:T(128)}, s32[2]{0:T(128)S(1)}, u32[]{:S(2)}) copy-start(s32[2]{0:T(128)S(1)} %pad_add_fusion.1.place) | copy-start | bytes 28
  34.7 36.0 %copy-start.2 = (s32[32,1,128]{2,1,0:T(1,128)}, s32[32,1,128]{2,1,0:T(1,128)S(1)}, u32[]{:S(2)}) copy-start(s32[32,1,128]{2,1,0:T(1,128)S(1)} %get-tuple-element.12) | copy-start | bytes 49156
  34.7 36.0 %copy-start.4 = (s32[32,1,128]{2,1,0:T(1,128)}, s32[32,1,128]{2,1,0:T(1,128)S(1)}, u32[]{:S(2)}) copy-start(s32[32,1,128]{2,1,0:T(1,128)S(1)} %get-tuple-element.13) | copy-start | bytes 49156
  68.7 2.0 copy-start.1
  70.7 7.7 %copy-start.8 = (s32[1024,3]{0,1:T(4,128)S(1)}, s32[1024,3]{0,1:T(4,128)}, u32[]{:S(2)}) copy-start(s32[1024,3]{0,1:T(4,128)} %param.9) | copy-start | bytes 36868
  70.7 58.5 %all-to-all-start = ((bf16[32,40,1600]{2,1,0:T(8,128)(2,1)}), bf16[32,40,1600]{2,1,0:T(8,128)(2,1)}, u32[]{:S(2)}, u32[]{:S(2)}) async-start(bf16[32,40,1600]{2,1,0:T(8,128)(2,1)} %copy-done.1), calls=%async_computation | async-start | bytes 8519680 | tf_op jit(solution)/shard_map/all_to_all | solution.py:390
  78.3 237.7 %reduce-scatter.2.cloned.1.call-start = ((), (), s32[]{:S(2)}) async-start(), calls=%async_computation.4 | async-start | bytes 5324800 | tf_op jit(solution)/shard_map/reduce_scatter | solution.py:401
  161.7 66.4 %copy-start.3 = (s32[32,1,128]{2,1,0:T(1,128)S(1)}, s32[32,1,128]{2,1,0:T(1,128)}, u32[]{:S(2)}) copy-start(s32[32,1,128]{2,1,0:T(1,128)} %copy-done.2) | copy-start | bytes 49156
  161.7 66.4 %copy-start.5 = (s32[32,1,128]{2,1,0:T(1,128)S(1)}, s32[32,1,128]{2,1,0:T(1,128)}, u32[]{:S(2)}) copy-start(s32[32,1,128]{2,1,0:T(1,128)} %copy-done.4) | copy-start | bytes 49156
  161.7 66.4 %copy-start.7 = (s32[2]{0:T(128)S(1)}, s32[2]{0:T(128)}, u32[]{:S(2)}) copy-start(s32[2]{0:T(128)} %copy-done.6) | copy-start | bytes 28
  234.3 2.0 copy-start
  236.3 0.7 copy-start.9
Sparse Core Ops, SparseCore 0:
  9.7 52.2 all-gather.2
  236.4 48.4 reduce-scatter.1

commit v2 on v1

v2 whole, which is shorter than its diff:
```python
import functools
import math

import jax
import jax.numpy as jnp
import ml_dtypes
import numpy as np
from jax import lax
from jax.experimental import pallas as pl
from jax.experimental.pallas import tpu as pltpu
from jax.sharding import PartitionSpec as P

BF16 = jnp.bfloat16
F32 = jnp.float32
VMEM = pl.BlockSpec(memory_space=pltpu.VMEM)
SMEM = pl.BlockSpec(memory_space=pltpu.SMEM)
EDGE = 40
AREA = 1600
ORB_DEV = 32
CAP = 4
SLOTS = 32
BATCH = 8
PADDED = 1792
TOP = 24
LEFT = 896
TILES = [(at, min(128, AREA - at)) for at in range(0, AREA, 128)]
CHUNKS = [(0, 256), (256, 256), (512, 384), (896, 384), (1280, 320)]
PEERS = 8
LEVELS = 4
MESH = pl.DeviceIdType.MESH
WIDE = [(at, min(256, AREA - at)) for at in range(0, AREA, 256)]


@functools.cache
def tables():
    number = np.arange(EDGE, dtype=np.float64) + 1.0
    sine = np.sqrt(2.0 / (EDGE + 1.0)) * np.sin(
        math.pi * number[:, None] * number[None, :] / (EDGE + 1.0)
    )
    sine32 = sine.astype(np.float32)
    plane = (sine32[:, None, :, None] * sine32[None, :, None, :]).reshape(AREA, AREA)
    plane = np.pad(plane, ((0, 0), (0, PADDED - AREA))).astype(ml_dtypes.bfloat16)
    eigen = 2.0 - 2.0 * np.cos(math.pi * number / (EDGE + 1.0))
    green = 1.0 / (eigen[:, None, None] + eigen[None, :, None] + eigen[None, None, :])
    green = np.pad(green.reshape(EDGE, AREA), ((0, 0), (0, PADDED - AREA)))
    green = np.tile(green.astype(np.float32), (2, 1))
    high = sine32.astype(ml_dtypes.bfloat16)
    low = (sine32 - high.astype(np.float32)).astype(ml_dtypes.bfloat16)
    two = np.eye(2, dtype=np.float32)
    pair_high = np.kron(two, high.astype(np.float32))
    pair_low = np.kron(two, low.astype(np.float32))
    sine_pair = np.concatenate([pair_high, pair_high, pair_low], 1).astype(ml_dtypes.bfloat16)
    along_z = np.tile(np.arange(1664, dtype=np.int32) % EDGE, (8, 1))
    return sine_pair, plane, green, along_z


def offset_class(level, a):
    return level if a < 4 else 3 - level


def peer_of(me, level, a):
    kind = offset_class(level, a)
    x = lax.rem(lax.div(me, 2) + 2 * (a % 2) + lax.rem(kind, 2), 4)
    y = lax.rem(lax.div(me, 8) + 2 * (a // 2 % 2) + lax.div(kind, 2), 4)
    return y * 8 + x * 2 + lax.rem(me + a // 4, 2)


def mirror_of(level, a):
    kind = offset_class(level, a)
    x = lax.rem(a % 2 + lax.rem(kind, 2), 2)
    y = lax.rem(a // 2 % 2 + lax.div(kind, 2), 2)
    return a // 4 * 4 + y * 2 + x


def selector(index_of):
    column = lax.broadcasted_iota(jnp.int32, (8, 256), 1)
    row = lax.broadcasted_iota(jnp.int32, (8, 256), 0)
    offset = column - row * ORB_DEV
    blocks = []
    for slot in range(SLOTS):
        index = index_of(slot // CAP, slot % CAP)
        index = jnp.where(index < 0, 100000, index)
        blocks.append((offset == index).astype(F32))
    return jnp.concatenate(blocks, 0)


def entry(row, at):
    lane = lax.broadcasted_iota(jnp.int32, (1, 128), 1)
    return jnp.sum(jnp.where(lane == at, row, 0), axis=1, keepdims=True)


def selectors(me, level, lists, mine):
    asked = selector(lambda a, c: entry(lists[level, a, 0:1, :], me * CAP + c))
    ahead = selector(lambda a, c: entry(mine[1:2, :], peer_of(me, level, a) * CAP + c))
    return asked, ahead


def greet(me, level):
    barrier = pltpu.get_barrier_semaphore()
    for a in range(1, PEERS):
        pl.semaphore_signal(
            barrier, inc=1, device_id=(peer_of(me, level, a), level), device_id_type=MESH
        )
    for step in range(1, LEVELS):
        pl.semaphore_signal(
            barrier, inc=1, device_id=(me, lax.rem(level + step, LEVELS)), device_id_type=MESH
        )

    @pl.when(level != 0)
    def _():
        pl.semaphore_signal(
            barrier, inc=1, device_id=(peer_of(me, level, 0), level), device_id_type=MESH
        )
        pl.semaphore_wait(barrier, PEERS + LEVELS - 1)

    @pl.when(level == 0)
    def _():
        pl.semaphore_wait(barrier, PEERS + LEVELS - 2)


class Exchange:
    def __init__(self, me, level, source, target, send, receive):
        self.level = level
        self.local = (source(0), target(0), send.at[0])
        self.copies = [
            pltpu.make_async_remote_copy(
                source(a),
                target(mirror_of(level, a)),
                send.at[a],
                receive.at[mirror_of(level, a)],
                device_id=(peer_of(me, level, a), level),
                device_id_type=MESH,
            )
            for a in range(PEERS)
        ]
        self.arrivals = [
            pltpu.make_async_remote_copy(
                source(a),
                target(a),
                send.at[a],
                receive.at[a],
                device_id=(peer_of(me, level, a), level),
                device_id_type=MESH,
            )
            for a in range(PEERS)
        ]

    def start(self):
        @pl.when(self.level != 0)
        def _():
            self.copies[0].start()

        @pl.when(self.level == 0)
        def _():
            pltpu.make_async_copy(*self.local).start()

        for copy in self.copies[1:]:
            copy.start()

    def wait_recv(self):
        @pl.when(self.level != 0)
        def _():
            self.arrivals[0].wait_recv()

        @pl.when(self.level == 0)
        def _():
            pltpu.make_async_copy(*self.local).wait()

        for copy in self.arrivals[1:]:
            copy.wait_recv()

    def wait_send(self):
        @pl.when(self.level != 0)
        def _():
            self.copies[0].wait_send()

        for copy in self.copies[1:]:
            copy.wait_send()


class Spread:
    def __init__(self, me, level, source, target, send, receive):
        self.copies = []
        for step in range(1, LEVELS):
            other = lax.rem(level + step, LEVELS)
            self.copies.append(
                pltpu.make_async_remote_copy(
                    source(other),
                    target(level),
                    send.at[step],
                    receive.at[step],
                    device_id=(me, other),
                    device_id_type=MESH,
                )
            )
        self.arrivals = []
        for step in range(1, LEVELS):
            other = lax.rem(level + LEVELS - step, LEVELS)
            self.arrivals.append(
                pltpu.make_async_remote_copy(
                    source(other),
                    target(other),
                    send.at[step],
                    receive.at[step],
                    device_id=(me, other),
                    device_id_type=MESH,
                )
            )

    def start(self):
        for copy in self.copies:
            copy.start()

    def wait_recv(self):
        for copy in self.arrivals:
            copy.wait_recv()

    def wait_send(self):
        for copy in self.copies:
            copy.wait_send()


def fetch_kernel(mine, own, *refs):
    count = len(CHUNKS)
    partners, phis, lists = refs[:count], refs[count : 2 * count], refs[2 * count]
    refs = refs[2 * count + 1 :]
    gathered, picked = refs[:count], refs[count : 2 * count]
    peer_send, peer_receive, level_send, level_receive = refs[2 * count :]
    me, level = lax.axis_index("orb"), lax.axis_index("grid")
    greet(me, level)
    spreads, exchanges = [], []
    for k, (at, width) in enumerate(CHUNKS):
        spreads.append(
            Spread(
                me, level,
                lambda other, at=at, width=width: own.at[:, :, pl.ds(at, width)],
                lambda other, k=k: gathered[k].at[other],
                level_send.at[k], level_receive.at[k],
            )
        )
        exchanges.append(
            Exchange(
                me, level,
                lambda a, k=k: picked[k].at[pl.ds(a * CAP, CAP)],
                lambda a, k=k: partners[k].at[pl.ds(a * CAP, CAP)],
                peer_send.at[k], peer_receive.at[k],
            )
        )
    near = Exchange(
        me, level, lambda a: mine, lambda a: lists.at[level, a],
        peer_send.at[count], peer_receive.at[count],
    )
    far = Spread(
        me, level, lambda other: lists.at[level], lambda other: lists.at[other],
        level_send.at[count], level_receive.at[count],
    )
    near.start()
    for spread in spreads:
        spread.start()
    for k, (at, width) in enumerate(CHUNKS):
        gathered[k][level] = own[:, :, at : at + width]
    near.wait_recv()
    far.start()
    asked, ahead = selectors(me, level, lists, mine)
    both = jnp.concatenate([asked, ahead], 0).astype(BF16)
    for k, (at, width) in enumerate(CHUNKS):
        spreads[k].wait_recv()
        planes = gathered[k].reshape(EDGE, ORB_DEV, width)
        for start in range(0, EDGE, 8):
            source = planes[start : start + 8].reshape(256, width)
            out = jnp.dot(both, source, preferred_element_type=F32).astype(BF16)
            out = out.reshape(2 * SLOTS, 8, width)
            picked[k][:, start : start + 8, :] = out[:SLOTS]
            phis[k][:, start : start + 8, :] = out[SLOTS:]
        exchanges[k].start()
    far.wait_recv()
    for exchange in exchanges:
        exchange.wait_recv()
    for part in [near, far] + spreads + exchanges:
        part.wait_send()


def give_back_kernel(mine, lists, energy, *refs):
    count = len(CHUNKS)
    products, own_terms = refs[:count], refs[count : 2 * count]
    total, energies = refs[2 * count : 2 * count + 2]
    refs = refs[2 * count + 2 :]
    returned, sums, slabs = refs[:count], refs[count : 2 * count], refs[2 * count : 3 * count]
    column, peer_send, peer_receive, level_send, level_receive = refs[3 * count :]
    me, level = lax.axis_index("orb"), lax.axis_index("grid")
    greet(me, level)
    spreads, exchanges = [], []
    for k in range(count):
        exchanges.append(
            Exchange(
                me, level,
                lambda a, k=k: products[k].at[pl.ds(a * CAP, CAP)],
                lambda a, k=k: returned[k].at[pl.ds(a * CAP, CAP)],
                peer_send.at[k], peer_receive.at[k],
            )
        )
        spreads.append(
            Spread(
                me, level,
                lambda other, k=k: sums[k].at[other],
                lambda other, k=k: slabs[k].at[other],
                level_send.at[k], level_receive.at[k],
            )
        )
    levels = Spread(
        me, level, lambda other: energy, lambda other: column.at[other],
        level_send.at[count], level_receive.at[count],
    )
    near = Exchange(
        me, level, lambda a: column, lambda a: energies.at[level, a],
        peer_send.at[count], peer_receive.at[count],
    )
    far = Spread(
        me, level, lambda other: energies.at[level], lambda other: energies.at[other],
        level_send.at[count + 1], level_receive.at[count + 1],
    )
    levels.start()
    for exchange in exchanges:
        exchange.start()
    column[level] = energy[...]
    asked, ahead = selectors(me, level, lists, mine)
    both = jnp.concatenate([asked, ahead], 0).T.astype(BF16)
    levels.wait_recv()
    near.start()
    for k, (at, width) in enumerate(CHUNKS):
        exchanges[k].wait_recv()
        planes = sums[k].reshape(EDGE, ORB_DEV, width)
        for start in range(0, EDGE, 8):
            rows = slice(start, start + 8)
            boxes = jnp.concatenate(
                [
                    returned[k][:, rows, :].reshape(256, width),
                    own_terms[k][:, rows, :].reshape(256, width),
                ],
                0,
            )
            out = jnp.dot(both, boxes, preferred_element_type=F32)
            planes[rows] = out.reshape(8, ORB_DEV, width).astype(BF16)
        spreads[k].start()
        if k == 0:
            near.wait_recv()
            far.start()
    for k, (at, width) in enumerate(CHUNKS):
        spreads[k].wait_recv()
        out = sums[k][level].astype(F32)
        for step in range(1, LEVELS):
            out = out + slabs[k][lax.rem(level + step, LEVELS)].astype(F32)
        total[:, :, at : at + width] = out
    far.wait_recv()
    for part in [levels, near, far] + spreads + exchanges:
        part.wait_send()


class TiledBoxes:
    def __init__(self, refs):
        self.refs = refs

    def at(self, slot, at, width):
        for ref, (start, size) in zip(self.refs, CHUNKS):
            if start <= at < start + size:
                return ref.at[slot, :, pl.ds(at - start, width)]

    def load(self, slot, at, width):
        return self.at(slot, at, width)[...].astype(F32)

    def store(self, slot, at, width, value):
        self.at(slot, at, width)[...] = value


def shift_tiles(pad, along_z, deltas, emit):
    dx, dy, dz = deltas
    start = LEFT + EDGE * dy + dz
    whole = lax.div(start, 128)
    part = start - whole * 128
    turn = lax.rem(128 - part, 128)
    lane = lax.broadcasted_iota(jnp.int32, (EDGE, 128), 1)
    from_here = lane < 128 - part
    rows = pl.ds(TOP + dx, EDGE)

    def turned(tile):
        return pltpu.roll(pad[whole + tile, rows, :], turn, 1)

    here = turned(0)
    for tile, (at, width) in enumerate(TILES):
        after = turned(tile + 1)
        out = jnp.where(from_here, here, after)
        z = along_z[:, at : at + 128] + dz
        inside = (z >= 0) & (z < EDGE)
        out = jnp.where(inside[None], out.reshape(EDGE // 8, 8, 128), 0.0).reshape(EDGE, 128)
        emit(at, width, out)
        here = after


def solve_kernel(place, mine, offset, *refs):
    count_of = len(CHUNKS)
    groups = [refs[n * count_of : (n + 1) * count_of] for n in range(2)]
    partners, phis = [TiledBoxes(group) for group in groups]
    sine_pair, plane, green, along_z = refs[2 * count_of : 2 * count_of + 4]
    refs = refs[2 * count_of + 4 :]
    groups = [refs[n * count_of : (n + 1) * count_of] for n in range(2)]
    returned, own_terms = [TiledBoxes(group) for group in groups]
    energies = refs[2 * count_of]
    refs = refs[2 * count_of + 1 :]
    live, places, pad, den, stack, forward, scaled, inverse, shifted, potential = refs
    me, level = place[0], place[1]
    for a in range(PEERS):
        places[a] = peer_of(me, level, a)

    def clear(at, _):
        energies[at] = 0.0
        return 0

    lax.fori_loop(0, 128, clear, 0)

    def place_of(slot):
        return places[lax.div(slot, CAP)] * CAP + lax.rem(slot, CAP)

    def compact(slot, count):
        alive = mine[place_of(slot)] >= 0

        @pl.when(alive)
        def _():
            live[count] = slot

        @pl.when(jnp.logical_not(alive))
        def _():
            for at, width in TILES:
                returned.store(slot, at, width, jnp.zeros((EDGE, width), BF16))
                own_terms.store(slot, at, width, jnp.zeros((EDGE, width), BF16))

        return count + alive.astype(jnp.int32)

    count = lax.fori_loop(0, SLOTS, compact, jnp.int32(0))
    pad[...] = jnp.zeros_like(pad)
    den[...] = jnp.zeros_like(den)

    def deltas_of(slot):
        at = place_of(slot)
        i = (me * ORB_DEV + mine[128 + at]) * 3
        j = (places[lax.div(slot, CAP)] * ORB_DEV + mine[at]) * 3
        return tuple(offset[i + axis] - offset[j + axis] for axis in range(3))

    def split(value):
        high = value.astype(BF16)
        return high, (value - high.astype(F32)).astype(BF16)

    def sine_product(cols):
        return jnp.dot(sine_pair[...], stack[:, cols], preferred_element_type=F32)

    def batch(index, _):
        base = index * BATCH
        pairs = lax.div(jnp.minimum(count - base, BATCH) + 1, 2)

        def before(pair, _):
            for side in range(2):
                position = base + pair * 2 + side
                rows = pl.ds(pl.multiple_of(pair * 80 + side * EDGE, 8), EDGE)

                @pl.when(position < count)
                def _():
                    slot = live[position]
                    for at, width in TILES:
                        pad[(LEFT + at) // 128, TOP : TOP + EDGE, :width] = partners.load(
                            slot, at, width
                        )

                    def emit(at, width, out):
                        shifted[rows, at : at + 128] = out
                        phi = phis.load(slot, at, width)
                        den[side * EDGE : (side + 1) * EDGE, at : at + width] = (
                            phi * out[:, :width]
                        )

                    shift_tiles(pad, along_z, deltas_of(slot), emit)

            for at, width in TILES:
                cols = slice(at, at + width)
                high, low = split(den[:, cols])
                stack[0:80, cols] = high
                stack[80:160, cols] = low
                stack[160:240, cols] = high
            rows = pl.ds(pl.multiple_of(pair * 80, 16), 80)
            for at, width in WIDE:
                cols = slice(at, at + width)
                forward[rows, cols] = sine_product(cols).astype(BF16)
            return 0

        lax.fori_loop(0, pairs, before, 0)

        def to_coeffs(step, _):
            cols = pl.ds(pl.multiple_of(step * 256, 256), 256)
            coeffs = jnp.dot(forward[...], plane[:, cols], preferred_element_type=F32)
            for pair in range(BATCH // 2):
                scaled[pair * 80 : pair * 80 + 80, cols] = (
                    green[:, cols] * coeffs[pair * 80 : pair * 80 + 80]
                ).astype(BF16)
            return 0

        lax.fori_loop(0, PADDED // 256, to_coeffs, 0)

        def to_inverse(step, _):
            cols = pl.ds(pl.multiple_of(step * 256, 256), 256)
            inverse[:, cols] = jnp.dot(
                scaled[:, :AREA], plane[:, cols], preferred_element_type=F32
            )
            return 0

        lax.fori_loop(0, PADDED // 256, to_inverse, 0)

        def after(pair, _):
            rows = pl.ds(pl.multiple_of(pair * 80, 16), 80)
            for at, width in TILES:
                cols = slice(at, at + width)
                high, low = split(inverse[rows, cols])
                stack[0:80, cols] = high
                stack[80:160, cols] = low
                stack[160:240, cols] = high
            for at, width in WIDE:
                cols = slice(at, at + width)
                potential[:, cols] = sine_product(cols)
            for side in range(2):
                position = base + pair * 2 + side
                half = pl.ds(pl.multiple_of(pair * 80 + side * EDGE, 8), EDGE)

                @pl.when(position < count)
                def _():
                    slot = live[position]
                    energy = jnp.zeros((EDGE, 128), F32)
                    for at, width in TILES:
                        cols = slice(at, at + width)
                        phi = phis.load(slot, at, width)
                        solved = potential[side * EDGE : (side + 1) * EDGE, cols]
                        term = solved * shifted[half, cols]
                        own_terms.store(slot, at, width, term.astype(BF16))
                        cell = term * phi
                        if width < 128:
                            cell = jnp.concatenate(
                                [cell, jnp.zeros((EDGE, 128 - width), F32)], 1
                            )
                        energy = energy + cell
                        pad[(LEFT + at) // 128, TOP : TOP + EDGE, :width] = (
                            (solved * phi).astype(BF16).astype(F32)
                        )
                    energies[place_of(slot)] = jnp.sum(energy) / (EDGE * EDGE * EDGE)

                    back = tuple(-delta for delta in deltas_of(slot))

                    def emit(at, width, out):
                        returned.store(slot, at, width, out[:, :width].astype(BF16))

                    shift_tiles(pad, along_z, back, emit)

            return 0

        lax.fori_loop(0, pairs, after, 0)
        return 0

    lax.fori_loop(0, lax.div(count + BATCH - 1, BATCH), batch, 0)


def gram_kernel(place, lists, energies, gram, half):
    orbitals = gram.shape[0]
    row = lax.broadcasted_iota(jnp.int32, (orbitals, 128), 0)
    slot = lax.broadcasted_iota(jnp.int32, (orbitals, 128), 1)
    owner_here = lax.div(row, ORB_DEV) == lax.div(slot, CAP)
    within = lax.rem(row, ORB_DEV)
    first_row = lax.broadcasted_iota(jnp.int32, (ORB_DEV, 128), 0)
    for a in range(PEERS):

        def owner(level, _):
            here = lists[level, a]
            energy = jnp.sum(energies[level, a], axis=0)
            second = (owner_here & (within == here[0:1])).astype(F32).astype(BF16)
            value = jnp.where(first_row == here[1:2], energy, 0.0)
            high = value.astype(BF16)
            rest = value - high.astype(F32)
            middle = rest.astype(BF16)
            low = (rest - middle.astype(F32)).astype(BF16)
            parts = jnp.concatenate([high, middle, low], 0)
            out = lax.dot_general(
                parts, second, (((1,), (1,)), ((), ())), preferred_element_type=F32
            )
            start = peer_of(place[0], level, a) * ORB_DEV
            rows = pl.ds(pl.multiple_of(start, ORB_DEV), ORB_DEV)
            half[rows, :] = out[0:32] + out[32:64] + out[64:96]
            return 0

        lax.fori_loop(0, LEVELS, owner, 0)
    for y in range(0, orbitals, 128):
        for x in range(0, orbitals, 128):
            gram[y : y + 128, x : x + 128] = (
                half[y : y + 128, x : x + 128] + half[x : x + 128, y : y + 128].T
            )


def params(mebibytes, **more):
    return pltpu.CompilerParams(vmem_limit_bytes=mebibytes * 2**20, **more)


BOXES = [jax.ShapeDtypeStruct((SLOTS, EDGE, width), BF16) for _, width in CHUNKS]
COUNT = len(CHUNKS)


def semaphores(extra):
    return [
        pltpu.SemaphoreType.DMA((COUNT + 1, PEERS)),
        pltpu.SemaphoreType.DMA((COUNT + 1, PEERS)),
        pltpu.SemaphoreType.DMA((COUNT + extra, LEVELS)),
        pltpu.SemaphoreType.DMA((COUNT + extra, LEVELS)),
    ]


def fetch(mine, own):
    slab = own.shape[0]
    outs = pl.pallas_call(
        fetch_kernel,
        out_shape=(*BOXES, *BOXES, jax.ShapeDtypeStruct((LEVELS, PEERS, 2, 128), jnp.int32)),
        in_specs=[VMEM] * 2,
        out_specs=(VMEM,) * (2 * COUNT + 1),
        scratch_shapes=[
            *[pltpu.VMEM((LEVELS, slab, ORB_DEV, width), BF16) for _, width in CHUNKS],
            *[pltpu.VMEM((SLOTS, EDGE, width), BF16) for _, width in CHUNKS],
            *semaphores(1),
        ],
        compiler_params=params(56, collective_id=1, has_side_effects=True),
        name="fetch",
    )(mine, own)
    return outs[:COUNT], outs[COUNT : 2 * COUNT], outs[2 * COUNT]


def solve(place, mine, offset, partners, phis):
    constants = [jnp.asarray(table) for table in tables()]
    outs = pl.pallas_call(
        solve_kernel,
        out_shape=(*BOXES, *BOXES, jax.ShapeDtypeStruct((128,), F32)),
        in_specs=[SMEM] * 3 + [VMEM] * (2 * COUNT + 4),
        out_specs=(VMEM,) * (2 * COUNT) + (SMEM,),
        scratch_shapes=[
            pltpu.SMEM((SLOTS + 8,), jnp.int32),
            pltpu.SMEM((PEERS,), jnp.int32),
            pltpu.VMEM((27, 88, 128), F32),
            pltpu.VMEM((80, 1664), F32),
            pltpu.VMEM((240, AREA), BF16),
            pltpu.VMEM((BATCH * EDGE, AREA), BF16),
            pltpu.VMEM((BATCH * EDGE, PADDED), BF16),
            pltpu.VMEM((BATCH * EDGE, PADDED), F32),
            pltpu.VMEM((BATCH * EDGE, 1664), F32),
            pltpu.VMEM((80, AREA), F32),
        ],
        compiler_params=params(58),
        name="solve",
    )(place, mine, offset, *partners, *phis, *constants)
    return outs[:COUNT], outs[COUNT : 2 * COUNT], outs[2 * COUNT]


def give_back(mine, lists, energy, products, own_terms, slab):
    return pl.pallas_call(
        give_back_kernel,
        out_shape=(
            jax.ShapeDtypeStruct((slab, ORB_DEV, AREA), F32),
            jax.ShapeDtypeStruct((LEVELS, PEERS, LEVELS, 1, 128), F32),
        ),
        in_specs=[VMEM] * (3 + 2 * COUNT),
        out_specs=(VMEM,) * 2,
        scratch_shapes=[
            *[pltpu.VMEM((SLOTS, EDGE, width), BF16) for _, width in CHUNKS],
            *[pltpu.VMEM((LEVELS, slab, ORB_DEV, width), BF16) for _, width in CHUNKS],
            *[pltpu.VMEM((LEVELS, slab, ORB_DEV, width), BF16) for _, width in CHUNKS],
            pltpu.VMEM((LEVELS, 1, 128), F32),
            *semaphores(2),
        ],
        compiler_params=params(56, collective_id=2, has_side_effects=True),
        name="give_back",
    )(mine, lists, energy, *products, *own_terms)


def gram_of(place, lists, energies, orbitals):
    return pl.pallas_call(
        gram_kernel,
        out_shape=jax.ShapeDtypeStruct((orbitals, orbitals), F32),
        in_specs=[SMEM, VMEM, VMEM],
        out_specs=VMEM,
        scratch_shapes=[pltpu.VMEM((orbitals, orbitals), F32)],
        compiler_params=params(32),
        name="gram",
    )(place, lists, energies)


def on_device(orbitals, box_offset, partner_slot, first_slot):
    place = jnp.stack([lax.axis_index("orb"), lax.axis_index("grid")]).astype(jnp.int32)
    mine = jnp.concatenate([partner_slot, first_slot], 0).reshape(2, -1)
    partners, phis, lists = fetch(mine, orbitals.transpose(1, 0, 2))
    products, own_terms, energy = solve(
        place, mine.reshape(-1), box_offset.reshape(-1), partners, phis
    )
    terms, energies = give_back(
        mine, lists, energy.reshape(1, -1), products, own_terms, orbitals.shape[1]
    )
    gram = gram_of(place, lists, energies, box_offset.shape[0])
    return (terms.transpose(1, 0, 2), gram)


def solution(mesh):
    placed = (P("orb", "grid", None), P(), P("orb", None, None), P("orb", None, None))
    return jax.shard_map(
        on_device,
        mesh=mesh,
        in_specs=placed,
        out_specs=(P("orb", "grid", None), P()),
        check_vma=False,
    )
```

time: 326 us -> 249 us (0.76)
  the two profiles are of different devices: /device:TPU:1 before, /device:TPU:66 now
where the time goes in v2:
time: 249 us; the launch traced here: 248 us
  Pallas kernels  241 us (97%)
  local copies, waits for them, and re-layouts  5.46 us (2%)
    pallas_call x1, Pallas kernels, give_back(): pl.pallas_call(give_back_kernel, out_shape=(jax.ShapeDtypeStruct((slab, O...  122 us
    pallas_call x1, Pallas kernels, fetch(): pl.pallas_call(fetch_kernel, out_shape=(*BOXES, *BOXES, jax.ShapeDtypeStr...  74.2 us
    pallas_call x1, Pallas kernels, solve(): pl.pallas_call(solve_kernel, out_shape=(*BOXES, *BOXES, jax.ShapeDtypeStr...  33.9 us
    pallas_call x1, Pallas kernels, gram_of(): pl.pallas_call(gram_kernel, out_shape=jax.ShapeDtypeStruct((orbitals, orb...  11.2 us

profile of v2, /device:TPU:66, one launch (start us, length us, event | category | flops | bytes accessed | tf_op | source)
XLA Modules:
  0.0 248.4 jit_solution(15200469135288165990)
XLA Ops:
  0.6 0.7 pad_add_fusion.1.place
  1.3 0.7 pad_add_fusion
  2.0 0.1 copy.11
  2.1 0.7 reshape.13.mine
  2.8 0.7 reshape_reshape.3.mine
  3.5 0.9 copy.13
  4.4 0.9 reshape.14.offset
  5.3 74.2 %fetch.1 = (bf16[32,40,256]{2,1,0:T(8,128)(2,1)}, bf16[32,40,256]{2,1,0:T(8,128)(2,1)}, bf16[32,40,384]{2,1,0:T(8,128)(2,1)}, bf16[32,40,384]{2,1,0:T(8,128)(2,1...) custom-call(s32[2,128]{1,0:T(2,128)} %reshape.13.mine, ...), custom_call_target="tpu_custom_call" | custom-call | tf_op jit(solution)/shard_map/fetch/pallas_call | solution.py:620
  79.5 33.9 %solve.1 = (bf16[32,40,256]{2,1,0:T(8,128)(2,1)}, bf16[32,40,256]{2,1,0:T(8,128)(2,1)}, bf16[32,40,384]{2,1,0:T(8,128)(2,1)}, bf16[32,40,384]{2,1,0:T(8,128)(2,1...) custom-call(s32[2]{0:T(128)} %pad_add_fusion.1.place, ...), custom_call_target="tpu_custom_call" | custom-call | tf_op jit(solution)/shard_map/solve/pallas_call | solution.py:638
  113.4 0.0 copy-start
  113.4 0.0 copy-start.2
  113.4 121.6 %give_back.1 = (f32[10,32,1600]{2,1,0:T(8,128)}, f32[4,8,4,1,128]{4,3,2,1,0:T(1,128)}) custom-call(s32[2,128]{1,0:T(2,128)} %reshape.13.mine, s32[4,8,2,128]{3,2,1,0:T(2,128)} %get-tuple-element.26.lists, f32[1,128]{1,0:T(1,128)} %bitcast.7, bf16[32,40,256]{2,1,0:T(8,128)(2,1)} %get-tuple-element.38.refs_0_, bf16[32,40,256]{2,1,0:T(8,128)(2,1)} %get-tuple-element.39.refs_1_, ...), custom_call_target="tpu_custom_call" | custom-call | tf_op jit(solution)/shard_map/give_back/pallas_call | solution.py:662
  235.0 0.0 copy-done
  235.1 0.0 copy-done.2
  235.1 0.0 copy-start.1
  235.1 0.8 copy-done.1
  235.9 0.0 copy-start.3
  235.9 11.2 %gram.1 = f32[1024,1024]{1,0:T(8,128)} custom-call(s32[2]{0:T(128)S(1)} %copy-done.2, s32[4,8,2,128]{3,2,1,0:T(2,128)S(1)} %copy-done, f32[4,8,4,1,128]{4,3,2,1,0:T(1,128)S(1)} %copy-done.1), custom_call_target="tpu_custom_call" | custom-call | tf_op jit(solution)/shard_map/gram/pallas_call | solution.py:683
  247.1 0.0 copy-done.3
  247.1 1.3 copy.15
Async XLA Ops:
  113.4 121.7 %copy-start = (s32[4,8,2,128]{3,2,1,0:T(2,128)S(1)}, s32[4,8,2,128]{3,2,1,0:T(2,128)}, u32[]{:S(2)}) copy-start(s32[4,8,2,128]{3,2,1,0:T(2,128)} %get-tuple-element.26.lists) | copy-start | bytes 98308
  113.4 121.7 %copy-start.2 = (s32[2]{0:T(128)S(1)}, s32[2]{0:T(128)}, u32[]{:S(2)}) copy-start(s32[2]{0:T(128)} %pad_add_fusion.1.place) | copy-start | bytes 28
  235.1 0.8 copy-start.1
  235.9 11.2 %copy-start.3 = (f32[10,32,1600]{2,1,0:T(8,128)S(1)}, f32[10,32,1600]{2,1,0:T(8,128)}, u32[]{:S(2)}) copy-start(f32[10,32,1600]{2,1,0:T(8,128)} %get-tuple-element.48) | copy-start | bytes 6144004

commit v3 on v1

v3 whole, which is shorter than its diff:
```python
import functools
import math

import jax
import jax.numpy as jnp
import ml_dtypes
import numpy as np
from jax import lax
from jax.experimental import pallas as pl
from jax.experimental.pallas import tpu as pltpu
from jax.sharding import PartitionSpec as P

BF16 = jnp.bfloat16
F32 = jnp.float32
VMEM = pl.BlockSpec(memory_space=pltpu.VMEM)
SMEM = pl.BlockSpec(memory_space=pltpu.SMEM)
EDGE = 40
AREA = 1600
ORB_DEV = 32
CAP = 4
SLOTS = 32
BATCH = 8
PADDED = 1792
STEP = 896
TOP = 24
LEFT = 896
TILES = [(at, min(128, AREA - at)) for at in range(0, AREA, 128)]
CHUNKS = [(0, 256), (256, 256), (512, 384), (896, 384), (1280, 320)]
COUNT = len(CHUNKS)
PEERS = 8
LEVELS = 4
MESH = pl.DeviceIdType.MESH
WIDE = [(at, min(256, AREA - at)) for at in range(0, AREA, 256)]


@functools.cache
def tables():
    number = np.arange(EDGE, dtype=np.float64) + 1.0
    sine = np.sqrt(2.0 / (EDGE + 1.0)) * np.sin(
        math.pi * number[:, None] * number[None, :] / (EDGE + 1.0)
    )
    sine32 = sine.astype(np.float32)
    plane = (sine32[:, None, :, None] * sine32[None, :, None, :]).reshape(AREA, AREA)
    plane = np.pad(plane, ((0, 0), (0, PADDED - AREA))).astype(ml_dtypes.bfloat16)
    eigen = 2.0 - 2.0 * np.cos(math.pi * number / (EDGE + 1.0))
    green = 1.0 / (eigen[:, None, None] + eigen[None, :, None] + eigen[None, None, :])
    green = np.pad(green.reshape(EDGE, AREA), ((0, 0), (0, PADDED - AREA)))
    green = np.tile(green.astype(np.float32), (2, 1))
    high = sine32.astype(ml_dtypes.bfloat16)
    low = (sine32 - high.astype(np.float32)).astype(ml_dtypes.bfloat16)
    two = np.eye(2, dtype=np.float32)
    pair_high = np.kron(two, high.astype(np.float32))
    pair_low = np.kron(two, low.astype(np.float32))
    sine_pair = np.concatenate([pair_high, pair_high, pair_low], 1).astype(ml_dtypes.bfloat16)
    along_z = np.tile(np.arange(1664, dtype=np.int32) % EDGE, (8, 1))
    return sine_pair, plane, green, along_z


def rem(value, by):
    return value % by if isinstance(value, int) else lax.rem(value, jnp.int32(by))


def div(value, by):
    return value // by if isinstance(value, int) else lax.div(value, jnp.int32(by))


def owner_at(me, level, r, sign):
    kind = level + div(r, 4) * (3 - 2 * level)
    x = rem(div(me, 2) + 8 + sign * (2 * rem(r, 2) + rem(kind, 2)), 4)
    y = rem(div(me, 8) + 8 + sign * (2 * rem(div(r, 2), 2) + div(kind, 2)), 4)
    return y * 8 + x * 2 + rem(me + div(r, 4), 2)


def peer_of(me, level, r):
    return owner_at(me, level, r, 1)


def asker_of(me, level, r):
    return owner_at(me, level, r, -1)


def selector(index_of):
    column = lax.broadcasted_iota(jnp.int32, (8, 256), 1)
    row = lax.broadcasted_iota(jnp.int32, (8, 256), 0)
    offset = column - row * ORB_DEV
    blocks = []
    for slot in range(SLOTS):
        index = index_of(slot // CAP, slot % CAP)
        index = jnp.where(index < 0, 100000, index)
        blocks.append((offset == index).astype(F32))
    return jnp.concatenate(blocks, 0)


def entry(row, at):
    lane = lax.broadcasted_iota(jnp.int32, (1, 128), 1)
    return jnp.sum(jnp.where(lane == at, row, 0), axis=1, keepdims=True)


def selectors(me, level, lists, mine):
    asked = selector(lambda r, c: entry(lists[level, r, 0:1, :], me * CAP + c))
    ahead = selector(lambda r, c: entry(mine[1:2, :], peer_of(me, level, r) * CAP + c))
    return asked, ahead


def greet(me, level):
    barrier = pltpu.get_barrier_semaphore()
    for a in range(1, PEERS):
        pl.semaphore_signal(
            barrier, inc=1, device_id=(peer_of(me, level, a), level), device_id_type=MESH
        )
    for step in range(1, LEVELS):
        pl.semaphore_signal(
            barrier, inc=1, device_id=(me, lax.rem(level + step, LEVELS)), device_id_type=MESH
        )

    @pl.when(level != 0)
    def _():
        pl.semaphore_signal(
            barrier, inc=1, device_id=(peer_of(me, level, 0), level), device_id_type=MESH
        )
        pl.semaphore_wait(barrier, PEERS + LEVELS - 1)

    @pl.when(level == 0)
    def _():
        pl.semaphore_wait(barrier, PEERS + LEVELS - 2)


class Exchange:
    def __init__(self, level, r, owner, source, target, send, receive):
        self.level, self.r = level, r
        self.remote = pltpu.make_async_remote_copy(
            source, target, send, receive, device_id=(owner, level), device_id_type=MESH
        )
        self.local = pltpu.make_async_copy(source, target, send) if r == 0 else None

    def both(self, remote, local):
        if self.r != 0:
            remote()
            return

        pl.when(self.level != 0)(remote)
        if local is not None:
            pl.when(self.level == 0)(local)

    def start(self):
        self.both(
            lambda: self.remote.start(), lambda: self.local.start()
        )

    def wait_recv(self):
        self.both(lambda: self.remote.wait_recv(), lambda: self.local.wait())

    def wait_send(self):
        self.both(lambda: self.remote.wait_send(), None)


class Spread:
    def __init__(self, me, level, source, target, send, receive):
        self.copies = []
        for step in range(1, LEVELS):
            other = lax.rem(level + step, LEVELS)
            self.copies.append(
                pltpu.make_async_remote_copy(
                    source(other),
                    target(level),
                    send.at[step],
                    receive.at[step],
                    device_id=(me, other),
                    device_id_type=MESH,
                )
            )
        self.arrivals = []
        for step in range(1, LEVELS):
            other = lax.rem(level + LEVELS - step, LEVELS)
            self.arrivals.append(
                pltpu.make_async_remote_copy(
                    source(other),
                    target(other),
                    send.at[step],
                    receive.at[step],
                    device_id=(me, other),
                    device_id_type=MESH,
                )
            )

    def start(self):
        for copy in self.copies:
            copy.start()

    def wait_recv(self):
        for copy in self.arrivals:
            copy.wait_recv()

    def wait_send(self):
        for copy in self.copies:
            copy.wait_send()


class TiledBoxes:
    def __init__(self, refs):
        self.refs = refs

    def at(self, slot, at, width):
        for ref, (start, size) in zip(self.refs, CHUNKS):
            if start <= at < start + size:
                return ref.at[slot, :, pl.ds(at - start, width)]

    def load(self, slot, at, width):
        return self.at(slot, at, width)[...].astype(F32)

    def store(self, slot, at, width, value):
        self.at(slot, at, width)[...] = value


def shift_tiles(pad, along_z, deltas, emit):
    dx, dy, dz = deltas
    start = LEFT + EDGE * dy + dz
    whole = lax.div(start, 128)
    part = start - whole * 128
    turn = lax.rem(128 - part, 128)
    lane = lax.broadcasted_iota(jnp.int32, (EDGE, 128), 1)
    from_here = lane < 128 - part
    rows = pl.ds(TOP + dx, EDGE)

    def turned(tile):
        return pltpu.roll(pad[whole + tile, rows, :], turn, 1)

    here = turned(0)
    for tile, (at, width) in enumerate(TILES):
        after = turned(tile + 1)
        out = jnp.where(from_here, here, after)
        z = along_z[:, at : at + 128] + dz
        inside = (z >= 0) & (z < EDGE)
        out = jnp.where(inside[None], out.reshape(EDGE // 8, 8, 128), 0.0).reshape(EDGE, 128)
        emit(at, width, out)
        here = after


def solve_group(me, level, group, mine, offset, partners, phis, tables, scratch, energy):
    partners, phis, returned, own_terms = [TiledBoxes(boxes) for boxes in (*partners, *phis)]
    sine_pair, plane, green, along_z = tables
    pad, den, stack, forward, scaled, inverse, shifted, potential = scratch

    def place_of(slot):
        return peer_of(me, level, div(slot, CAP)) * CAP + rem(slot, CAP)

    def deltas_of(slot):
        at = place_of(slot)
        i = (me * ORB_DEV + jnp.maximum(mine[128 + at], 0)) * 3
        j = (peer_of(me, level, div(slot, CAP)) * ORB_DEV + jnp.maximum(mine[at], 0)) * 3
        return tuple(offset[i + axis] - offset[j + axis] for axis in range(3))

    def split(value):
        high = value.astype(BF16)
        return high, (value - high.astype(F32)).astype(BF16)

    def sine_product(cols):
        return jnp.dot(sine_pair[...], stack[:, cols], preferred_element_type=F32)

    def before(pair, _):
        for side in range(2):
            slot = group * BATCH + pair * 2 + side
            rows = pl.ds(pl.multiple_of(pair * 80 + side * EDGE, 8), EDGE)
            for at, width in TILES:
                pad[(LEFT + at) // 128, TOP : TOP + EDGE, :width] = partners.load(
                    slot, at, width
                )

            def emit(at, width, out):
                shifted[rows, at : at + 128] = out
                phi = phis.load(slot, at, width)
                den[side * EDGE : (side + 1) * EDGE, at : at + width] = phi * out[:, :width]

            shift_tiles(pad, along_z, deltas_of(slot), emit)
        for at, width in TILES:
            cols = slice(at, at + width)
            high, low = split(den[:, cols])
            stack[0:80, cols] = high
            stack[80:160, cols] = low
            stack[160:240, cols] = high
        rows = pl.ds(pl.multiple_of(pair * 80, 16), 80)
        for at, width in WIDE:
            cols = slice(at, at + width)
            forward[rows, cols] = sine_product(cols).astype(BF16)
        return 0

    lax.fori_loop(0, BATCH // 2, before, 0)

    def to_coeffs(step, _):
        cols = pl.ds(pl.multiple_of(step * STEP, 128), STEP)
        coeffs = jnp.dot(forward[...], plane[:, cols], preferred_element_type=F32)
        for pair in range(BATCH // 2):
            scaled[pair * 80 : pair * 80 + 80, cols] = (
                green[:, cols] * coeffs[pair * 80 : pair * 80 + 80]
            ).astype(BF16)
        return 0

    lax.fori_loop(0, PADDED // STEP, to_coeffs, 0)

    def to_inverse(step, _):
        cols = pl.ds(pl.multiple_of(step * STEP, 128), STEP)
        inverse[:, cols] = jnp.dot(
            scaled[:, :AREA], plane[:, cols], preferred_element_type=F32
        )
        return 0

    lax.fori_loop(0, PADDED // STEP, to_inverse, 0)

    def after(pair, _):
        rows = pl.ds(pl.multiple_of(pair * 80, 16), 80)
        for at, width in TILES:
            cols = slice(at, at + width)
            high, low = split(inverse[rows, cols])
            stack[0:80, cols] = high
            stack[80:160, cols] = low
            stack[160:240, cols] = high
        for at, width in WIDE:
            cols = slice(at, at + width)
            potential[:, cols] = sine_product(cols)
        for side in range(2):
            slot = group * BATCH + pair * 2 + side
            half = pl.ds(pl.multiple_of(pair * 80 + side * EDGE, 8), EDGE)
            cells = jnp.zeros((EDGE, 128), F32)
            for at, width in TILES:
                cols = slice(at, at + width)
                phi = phis.load(slot, at, width)
                solved = potential[side * EDGE : (side + 1) * EDGE, cols]
                term = solved * shifted[half, cols]
                own_terms.store(slot, at, width, term.astype(BF16))
                cell = term * phi
                if width < 128:
                    cell = jnp.concatenate([cell, jnp.zeros((EDGE, 128 - width), F32)], 1)
                cells = cells + cell
                pad[(LEFT + at) // 128, TOP : TOP + EDGE, :width] = (
                    (solved * phi).astype(BF16).astype(F32)
                )
            value = jnp.sum(jnp.sum(cells, axis=0, keepdims=True), axis=1, keepdims=True)
            lane = lax.broadcasted_iota(jnp.int32, (1, 128), 1)
            energy[...] += jnp.where(
                lane == place_of(slot), value / (EDGE * EDGE * EDGE), 0.0
            )
            back = tuple(-delta for delta in deltas_of(slot))

            def emit(at, width, out):
                returned.store(slot, at, width, out[:, :width].astype(BF16))

            shift_tiles(pad, along_z, back, emit)
        return 0

    lax.fori_loop(0, BATCH // 2, after, 0)


def add_gram(me, lists, energies, gram, half):
    orbitals = gram.shape[0]
    row = lax.broadcasted_iota(jnp.int32, (orbitals, 128), 0)
    slot = lax.broadcasted_iota(jnp.int32, (orbitals, 128), 1)
    owner_here = lax.div(row, ORB_DEV) == lax.div(slot, CAP)
    within = lax.rem(row, ORB_DEV)
    first_row = lax.broadcasted_iota(jnp.int32, (ORB_DEV, 128), 0)

    def owner(index, _):
        level, r = div(index, PEERS), rem(index, PEERS)
        here = lists[level, r]
        energy = jnp.sum(energies[level, r], axis=0)
        second = (owner_here & (within == here[0:1])).astype(F32).astype(BF16)
        value = jnp.where(first_row == here[1:2], energy, 0.0)
        high = value.astype(BF16)
        rest = value - high.astype(F32)
        middle = rest.astype(BF16)
        low = (rest - middle.astype(F32)).astype(BF16)
        parts = jnp.concatenate([high, middle, low], 0)
        out = lax.dot_general(
            parts, second, (((1,), (1,)), ((), ())), preferred_element_type=F32
        )
        rows = pl.ds(pl.multiple_of(asker_of(me, level, r) * ORB_DEV, ORB_DEV), ORB_DEV)
        half[rows, :] = out[0:32] + out[32:64] + out[64:96]
        return 0

    lax.fori_loop(0, LEVELS * PEERS, owner, 0)
    for y in range(0, orbitals, 128):
        for x in range(0, orbitals, 128):
            gram[y : y + 128, x : x + 128] = (
                half[y : y + 128, x : x + 128] + half[x : x + 128, y : y + 128].T
            )


def exchange_kernel(
    mine_scalars, offset, mine, own, sine_pair, plane_source, green, along_z,
    total, gram, *refs,
):
    count = COUNT
    gathered, picked, partners, phis, returned, slabs = [
        refs[n * count : (n + 1) * count] for n in range(6)
    ]
    sums, products, own_terms = gathered, picked, partners
    refs = refs[6 * count :]
    lists, energy, column, energies, half, plane = refs[:6]
    scratch = refs[6:14]
    list_send, list_receive, out_send, out_receive, back_send, back_receive = refs[14:20]
    value_send, value_receive, level_send, level_receive, plane_sem = refs[20:]
    me, level = lax.axis_index("orb"), lax.axis_index("grid")

    out, back, near, values = [], [], [], []
    for r in range(PEERS):
        block = pl.ds(r * CAP, CAP)
        asker, peer = asker_of(me, level, r), peer_of(me, level, r)
        out.append([
            Exchange(level, r, asker, picked[k].at[block], partners[k].at[block],
                     out_send.at[k, r], out_receive.at[k, r])
            for k in range(count)
        ])
        back.append([
            Exchange(level, r, peer, products[k].at[block], returned[k].at[block],
                     back_send.at[k, r], back_receive.at[k, r])
            for k in range(count)
        ])
        near.append(
            Exchange(level, r, peer, mine, lists.at[level, r],
                     list_send.at[r], list_receive.at[r])
        )
        values.append(
            Exchange(level, r, peer, column, energies.at[level, r],
                     value_send.at[r], value_receive.at[r])
        )
    gathers, scatters = [], []
    for k, (at, width) in enumerate(CHUNKS):
        gathers.append(
            Spread(
                me, level,
                lambda other, at=at, width=width: own.at[:, :, pl.ds(at, width)],
                lambda other, k=k: gathered[k].at[other],
                level_send.at[k], level_receive.at[k],
            )
        )
        scatters.append(
            Spread(
                me, level,
                lambda other, k=k: sums[k].at[other],
                lambda other, k=k: slabs[k].at[other],
                level_send.at[count + k], level_receive.at[count + k],
            )
        )
    far = Spread(
        me, level, lambda other: lists.at[level], lambda other: lists.at[other],
        level_send.at[2 * count], level_receive.at[2 * count],
    )
    levels = Spread(
        me, level, lambda other: energy, lambda other: column.at[other],
        level_send.at[2 * count + 1], level_receive.at[2 * count + 1],
    )
    far_values = Spread(
        me, level, lambda other: energies.at[level], lambda other: energies.at[other],
        level_send.at[2 * count + 2], level_receive.at[2 * count + 2],
    )
    load_plane = pltpu.make_async_copy(plane_source, plane, plane_sem)

    load_plane.start()
    greet(me, level)
    for copy in near:
        copy.start()
    for gather in gathers:
        gather.start()
    for k, (at, width) in enumerate(CHUNKS):
        gathered[k][level] = own[:, :, at : at + width]
    energy[...] = jnp.zeros_like(energy)
    scratch[0][...] = jnp.zeros_like(scratch[0])
    for copy in near:
        copy.wait_recv()
    far.start()
    asked, ahead = selectors(me, level, lists, mine)
    both = jnp.concatenate([asked, ahead], 0).astype(BF16)

    def send_out(rs, k):
        if 0 <= k < count:
            for r in rs:
                out[r][k].start()

    for k, (at, width) in enumerate(CHUNKS):
        gathers[k].wait_recv()
        planes = gathered[k].reshape(EDGE, ORB_DEV, width)
        for start in range(0, EDGE, 8):
            source = planes[start : start + 8].reshape(256, width)
            boxes = jnp.dot(both, source, preferred_element_type=F32).astype(BF16)
            boxes = boxes.reshape(2 * SLOTS, 8, width)
            picked[k][:, start : start + 8, :] = boxes[:SLOTS]
            phis[k][:, start : start + 8, :] = boxes[SLOTS:]
        send_out(range(4), k)
        send_out(range(4, PEERS), k - 1)
    send_out(range(4, PEERS), count - 1)
    far.wait_recv()
    load_plane.wait()

    for group in range(LEVELS):
        rs = (2 * group, 2 * group + 1)
        for r in rs:
            for k in range(count):
                out[r][k].wait_recv()
                out[r][k].wait_send()
        solve_group(
            me, level, group, mine_scalars, offset,
            (partners, phis), (products, own_terms),
            (sine_pair, plane, green, along_z), scratch, energy,
        )
        for k in range(count):
            if group < 2 or k < 2:
                for r in rs:
                    back[r][k].start()
    levels.start()
    column[level] = energy[...]
    back_select = jnp.concatenate([asked, ahead], 0).T.astype(BF16)
    levels.wait_recv()
    for copy in values:
        copy.start()
    for k, (at, width) in enumerate(CHUNKS):
        for r in range(PEERS):
            back[r][k].wait_recv()
        if k + 2 < count:
            for r in range(4, PEERS):
                back[r][k + 2].start()
        planes = sums[k].reshape(EDGE, ORB_DEV, width)
        for start in range(0, EDGE, 8):
            rows = slice(start, start + 8)
            boxes = jnp.concatenate(
                [
                    returned[k][:, rows, :].reshape(256, width),
                    own_terms[k][:, rows, :].reshape(256, width),
                ],
                0,
            )
            slab = jnp.dot(back_select, boxes, preferred_element_type=F32)
            planes[rows] = slab.reshape(8, ORB_DEV, width).astype(BF16)
        scatters[k].start()
        if k == 0:
            for copy in values:
                copy.wait_recv()
            far_values.start()
    far_values.wait_recv()
    add_gram(me, lists, energies, gram, half)
    for k, (at, width) in enumerate(CHUNKS):
        scatters[k].wait_recv()
        slab = sums[k][level].astype(F32)
        for step in range(1, LEVELS):
            slab = slab + slabs[k][lax.rem(level + step, LEVELS)].astype(F32)
        total[:, :, at : at + width] = slab
    for copy in near + values + [copy for copies in back for copy in copies]:
        copy.wait_send()
    for spread in [far, levels, far_values] + gathers + scatters:
        spread.wait_send()


def params(mebibytes, **more):
    return pltpu.CompilerParams(vmem_limit_bytes=mebibytes * 2**20, **more)


def exchange(mine, offset, own):
    slab, orbitals = own.shape[0], offset.shape[0] // 3
    constants = [jnp.asarray(table) for table in tables()]
    boxes = [pltpu.VMEM((SLOTS, EDGE, width), BF16) for _, width in CHUNKS]
    slabs = [pltpu.VMEM((LEVELS, slab, ORB_DEV, width), BF16) for _, width in CHUNKS]
    any_place = pl.BlockSpec(memory_space=pl.ANY)
    dma = pltpu.SemaphoreType.DMA
    return pl.pallas_call(
        exchange_kernel,
        out_shape=(
            jax.ShapeDtypeStruct((slab, ORB_DEV, AREA), F32),
            jax.ShapeDtypeStruct((orbitals, orbitals), F32),
        ),
        in_specs=[SMEM, SMEM, VMEM, VMEM, VMEM, any_place, VMEM, VMEM],
        out_specs=(VMEM,) * 2,
        scratch_shapes=[
            *slabs, *boxes, *boxes, *boxes, *boxes, *slabs,
            pltpu.VMEM((LEVELS, PEERS, 2, 128), jnp.int32),
            pltpu.VMEM((1, 128), F32),
            pltpu.VMEM((LEVELS, 1, 128), F32),
            pltpu.VMEM((LEVELS, PEERS, LEVELS, 1, 128), F32),
            pltpu.VMEM((orbitals, orbitals), F32),
            pltpu.VMEM((AREA, PADDED), BF16),
            pltpu.VMEM((27, 88, 128), F32),
            pltpu.VMEM((80, 1664), F32),
            pltpu.VMEM((240, AREA), BF16),
            pltpu.VMEM((BATCH * EDGE, AREA), BF16),
            pltpu.VMEM((BATCH * EDGE, PADDED), BF16),
            pltpu.VMEM((BATCH * EDGE, PADDED), F32),
            pltpu.VMEM((BATCH * EDGE, 1664), F32),
            pltpu.VMEM((80, AREA), F32),
            dma((PEERS,)), dma((PEERS,)),
            dma((COUNT, PEERS)), dma((COUNT, PEERS)),
            dma((COUNT, PEERS)), dma((COUNT, PEERS)),
            dma((PEERS,)), dma((PEERS,)),
            dma((2 * COUNT + 3, LEVELS)), dma((2 * COUNT + 3, LEVELS)),
            dma(()),
        ],
        compiler_params=params(62, collective_id=1, has_side_effects=True),
        name="exchange",
    )(mine.reshape(-1), offset, mine, own, *constants)


def on_device(orbitals, box_offset, partner_slot, first_slot):
    mine = jnp.concatenate([partner_slot, first_slot], 0).reshape(2, -1)
    terms, gram = exchange(mine, box_offset.reshape(-1), orbitals.transpose(1, 0, 2))
    return (terms.transpose(1, 0, 2), gram)


def solution(mesh):
    placed = (P("orb", "grid", None), P(), P("orb", None, None), P("orb", None, None))
    return jax.shard_map(
        on_device,
        mesh=mesh,
        in_specs=placed,
        out_specs=(P("orb", "grid", None), P()),
        check_vma=False,
    )
```

time: 326 us -> 192 us (0.59)
  the two profiles are of different devices: /device:TPU:1 before, /device:TPU:86 now
where the time goes in v3:
time: 192 us
  Pallas kernels  182 us (95%)
  local copies, waits for them, and re-layouts  8.53 us (4%)
    pallas_call x1, Pallas kernels, exchange(): pl.pallas_call(exchange_kernel, out_shape=(jax.ShapeDtypeStruct((slab, OR...  182 us
    unnamed x5, local copies, waits for them, and re-layouts  6.19 us

profile of v3, /device:TPU:86, one launch (start us, length us, event | category | flops | bytes accessed | tf_op | source)
XLA Modules:
  0.0 192.1 jit_solution(16182682398765503030)
XLA Ops:
  0.6 0.7 pad_add_fusion
  1.3 0.1 copy.11
  1.4 0.7 reshape.11.mine
  2.1 0.7 reshape_reshape.3.mine_scalars
  2.8 0.9 copy.12
  3.7 0.9 reshape.10.offset
  4.6 182.2 %exchange.1 = (f32[10,32,1600]{2,1,0:T(8,128)}, f32[1024,1024]{1,0:T(8,128)}) custom-call(s32[256]{0:T(256)} %reshape_reshape.3.mine_scalars, s32[3072]{0:T(1024)} %reshape.10.offset, s32[2,128]{1,0:T(2,128)} %reshape.11.mine, bf16[10,32,1600]{2,1,0:T(8,128)(2,1)} %bitcast.3, bf16[80,240]{1,0:T(8,128)(2,1)} %constant.8.clone.sine_pair, ...), custom_call_target="tpu_custom_call" | custom-call | tf_op jit(solution)/shard_map/exchange/pallas_call | solution.py:562
  186.9 0.0 copy-start
  186.9 3.2 %copy.16 = f32[32,10,1600]{2,0,1:T(8,128)} copy(f32[32,10,1600]{2,0,1:T(8,128)} %bitcast.2) | data formatting | bytes 4096000
  190.1 0.0 copy-done
  190.1 2.0 %copy.17 = f32[1024,1024]{1,0:T(8,128)} copy(f32[1024,1024]{1,0:T(8,128)S(1)} %copy-done) | data formatting | bytes 8388608
Async XLA Ops:
  186.9 3.3 %copy-start = (f32[1024,1024]{1,0:T(8,128)S(1)}, f32[1024,1024]{1,0:T(8,128)}, u32[]{:S(2)}) copy-start(f32[1024,1024]{1,0:T(8,128)} %get-tuple-element.9) | copy-start | bytes 12582916

commit v4 on v3

--- a/solution.py
+++ b/solution.py
@@ -22,10 +22,14 @@
 BATCH = 8
 PADDED = 1792
 STEP = 896
+AHEAD = 2
+LAGS = (0,0,1,2)
+AT_ONCE = (5,5,3,3)
 TOP = 24
 LEFT = 896
 TILES = [(at, min(128, AREA - at)) for at in range(0, AREA, 128)]
-CHUNKS = [(0, 256), (256, 256), (512, 384), (896, 384), (1280, 320)]
+WIDTHS = (256, 256, 384, 384, 320)
+CHUNKS = [(sum(WIDTHS[:k]), width) for k, width in enumerate(WIDTHS)]
 COUNT = len(CHUNKS)
 PEERS = 8
 LEVELS = 4
@@ -152,6 +156,104 @@
 
     def wait_send(self):
         self.both(lambda: self.remote.wait_send(), None)
+
+
+def hop(me, level, step, source, target, send, receive):
+    return pltpu.make_async_remote_copy(
+        source, target, send, receive,
+        device_id=(me, lax.rem(level + step, LEVELS)), device_id_type=MESH,
+    )
+
+
+class RingGather:
+    def __init__(self, me, level, own, gathered, send, receive):
+        half = own.shape[0] // 2
+        low, high = pl.ds(0, half), pl.ds(half, half)
+        below, above = lax.rem(level + 3, LEVELS), lax.rem(level + 1, LEVELS)
+        opposite = lax.rem(level + 2, LEVELS)
+
+        def make(step, source, target, n):
+            return hop(me, level, step, source, target, send.at[n], receive.at[n])
+
+        self.near = [
+            make(1, own, gathered.at[level], 0),
+            make(3, own, gathered.at[level], 1),
+        ]
+        self.near_in = [
+            make(1, own, gathered.at[below], 0),
+            make(3, own, gathered.at[above], 1),
+        ]
+        self.far = [
+            make(1, gathered.at[below, low], gathered.at[below, low], 2),
+            make(3, gathered.at[above, high], gathered.at[above, high], 3),
+        ]
+        self.far_in = [
+            make(1, gathered.at[below, low], gathered.at[opposite, low], 2),
+            make(3, gathered.at[above, high], gathered.at[opposite, high], 3),
+        ]
+
+    def start(self):
+        for copy in self.near:
+            copy.start()
+
+    def forward(self):
+        for arrived, copy in zip(self.near_in, self.far):
+            arrived.wait_recv()
+            copy.start()
+
+    def wait_recv(self):
+        for copy in self.far_in:
+            copy.wait_recv()
+
+    def wait_send(self):
+        for copy in self.near + self.far:
+            copy.wait_send()
+
+
+class RingScatter:
+    def __init__(self, me, level, sums, far, near, send, receive):
+        self.sums, self.far_slabs, self.near_slabs, self.level = sums, far, near, level
+        half = sums.shape[1] // 2
+        low, high = pl.ds(0, half), pl.ds(half, half)
+        below, above = lax.rem(level + 3, LEVELS), lax.rem(level + 1, LEVELS)
+        opposite = lax.rem(level + 2, LEVELS)
+
+        def make(step, source, target, n):
+            return hop(me, level, step, source, target, send.at[n], receive.at[n])
+
+        self.far = [
+            make(1, sums.at[opposite, low], far.at[0], 0),
+            make(3, sums.at[opposite, high], far.at[1], 1),
+        ]
+        self.near = [
+            make(1, sums.at[above], near.at[0], 2),
+            make(3, sums.at[below], near.at[1], 3),
+        ]
+        self.places = [sums.at[above, low], sums.at[below, high]]
+
+    def start(self):
+        for copy in self.far:
+            copy.start()
+
+    def forward(self):
+        for n in range(2):
+            self.far[n].wait_recv()
+            place = self.places[n]
+            place[...] = (
+                place[...].astype(F32) + self.far_slabs[n].astype(F32)
+            ).astype(BF16)
+            self.near[n].start()
+
+    def result(self):
+        for copy in self.near:
+            copy.wait_recv()
+        near = self.near_slabs
+        mine = self.sums[self.level].astype(F32)
+        return mine + near[0].astype(F32) + near[1].astype(F32)
+
+    def wait_send(self):
+        for copy in self.far + self.near:
+            copy.wait_send()
 
 
 class Spread:
@@ -246,9 +348,10 @@
 
     def deltas_of(slot):
         at = place_of(slot)
-        i = (me * ORB_DEV + jnp.maximum(mine[128 + at], 0)) * 3
-        j = (peer_of(me, level, div(slot, CAP)) * ORB_DEV + jnp.maximum(mine[at], 0)) * 3
-        return tuple(offset[i + axis] - offset[j + axis] for axis in range(3))
+        partner, first = mine
+        i = me * ORB_DEV + jnp.maximum(first[0, at], 0)
+        j = peer_of(me, level, div(slot, CAP)) * ORB_DEV + jnp.maximum(partner[0, at], 0)
+        return tuple(offset[axis, i] - offset[axis, j] for axis in range(3))
 
     def split(value):
         high = value.astype(BF16)
@@ -385,19 +488,20 @@
 
 
 def exchange_kernel(
-    mine_scalars, offset, mine, own, sine_pair, plane_source, green, along_z,
-    total, gram, *refs,
+    partner, first, offset, partner_row, first_row, own, sine_pair, plane_source, green,
+    along_z, total_out, gram_out, *refs,
 ):
     count = COUNT
-    gathered, picked, partners, phis, returned, slabs = [
-        refs[n * count : (n + 1) * count] for n in range(6)
+    gathered, picked, partners, phis, returned, far_slabs, near_slabs = [
+        refs[n * count : (n + 1) * count] for n in range(7)
     ]
     sums, products, own_terms = gathered, picked, partners
-    refs = refs[6 * count :]
+    refs = refs[7 * count :]
     lists, energy, column, energies, half, plane = refs[:6]
     scratch = refs[6:14]
-    list_send, list_receive, out_send, out_receive, back_send, back_receive = refs[14:20]
-    value_send, value_receive, level_send, level_receive, plane_sem = refs[20:]
+    total, gram, mine = refs[14:17]
+    list_send, list_receive, out_send, out_receive, back_send, back_receive = refs[17:23]
+    value_send, value_receive, level_send, level_receive, plane_sem, result_sem = refs[23:]
     me, level = lax.axis_index("orb"), lax.axis_index("grid")
 
     out, back, near, values = [], [], [], []
@@ -425,18 +529,14 @@
     gathers, scatters = [], []
     for k, (at, width) in enumerate(CHUNKS):
         gathers.append(
-            Spread(
-                me, level,
-                lambda other, at=at, width=width: own.at[:, :, pl.ds(at, width)],
-                lambda other, k=k: gathered[k].at[other],
+            RingGather(
+                me, level, own.at[:, :, pl.ds(at, width)], gathered[k],
                 level_send.at[k], level_receive.at[k],
             )
         )
         scatters.append(
-            Spread(
-                me, level,
-                lambda other, k=k: sums[k].at[other],
-                lambda other, k=k: slabs[k].at[other],
+            RingScatter(
+                me, level, sums[k], far_slabs[k], near_slabs[k],
                 level_send.at[count + k], level_receive.at[count + k],
             )
         )
@@ -455,10 +555,12 @@
     load_plane = pltpu.make_async_copy(plane_source, plane, plane_sem)
 
     load_plane.start()
+    mine[0:1, :] = partner_row[...]
+    mine[1:2, :] = first_row[...]
     greet(me, level)
     for copy in near:
         copy.start()
-    for gather in gathers:
+    for gather in gathers[:AHEAD]:
         gather.start()
     for k, (at, width) in enumerate(CHUNKS):
         gathered[k][level] = own[:, :, at : at + width]
@@ -467,6 +569,14 @@
     for copy in near:
         copy.wait_recv()
     far.start()
+
+    def step_gather(k):
+        if k < count:
+            gathers[k].forward()
+        if k + AHEAD < count:
+            gathers[k + AHEAD].start()
+
+    step_gather(0)
     asked, ahead = selectors(me, level, lists, mine)
     both = jnp.concatenate([asked, ahead], 0).astype(BF16)
 
@@ -476,6 +586,7 @@
                 out[r][k].start()
 
     for k, (at, width) in enumerate(CHUNKS):
+        step_gather(k + 1)
         gathers[k].wait_recv()
         planes = gathered[k].reshape(EDGE, ORB_DEV, width)
         for start in range(0, EDGE, 8):
@@ -484,9 +595,11 @@
             boxes = boxes.reshape(2 * SLOTS, 8, width)
             picked[k][:, start : start + 8, :] = boxes[:SLOTS]
             phis[k][:, start : start + 8, :] = boxes[SLOTS:]
-        send_out(range(4), k)
-        send_out(range(4, PEERS), k - 1)
-    send_out(range(4, PEERS), count - 1)
+        for group, lag in enumerate(LAGS):
+            send_out((2 * group, 2 * group + 1), k - lag)
+    for k in range(count, count + max(LAGS)):
+        for group, lag in enumerate(LAGS):
+            send_out((2 * group, 2 * group + 1), k - lag)
     far.wait_recv()
     load_plane.wait()
 
@@ -497,14 +610,16 @@
                 out[r][k].wait_recv()
                 out[r][k].wait_send()
         solve_group(
-            me, level, group, mine_scalars, offset,
+            me, level, group, (partner, first), offset,
             (partners, phis), (products, own_terms),
             (sine_pair, plane, green, along_z), scratch, energy,
         )
         for k in range(count):
-            if group < 2 or k < 2:
+            if k < AT_ONCE[group]:
                 for r in rs:
                     back[r][k].start()
+    for gather in gathers:
+        gather.wait_send()
     levels.start()
     column[level] = energy[...]
     back_select = jnp.concatenate([asked, ahead], 0).T.astype(BF16)
@@ -514,8 +629,8 @@
     for k, (at, width) in enumerate(CHUNKS):
         for r in range(PEERS):
             back[r][k].wait_recv()
-        if k + 2 < count:
-            for r in range(4, PEERS):
+        for r in range(PEERS):
+            if AT_ONCE[r // 2] <= k + 2 < count:
                 back[r][k + 2].start()
         planes = sums[k].reshape(EDGE, ORB_DEV, width)
         for start in range(0, EDGE, 8):
@@ -530,21 +645,29 @@
             slab = jnp.dot(back_select, boxes, preferred_element_type=F32)
             planes[rows] = slab.reshape(8, ORB_DEV, width).astype(BF16)
         scatters[k].start()
+        if k > 0:
+            scatters[k - 1].forward()
         if k == 0:
             for copy in values:
                 copy.wait_recv()
             far_values.start()
+    scatters[count - 1].forward()
     far_values.wait_recv()
     add_gram(me, lists, energies, gram, half)
+    results = [pltpu.make_async_copy(gram, gram_out, result_sem.at[count])]
+    results[0].start()
     for k, (at, width) in enumerate(CHUNKS):
-        scatters[k].wait_recv()
-        slab = sums[k][level].astype(F32)
-        for step in range(1, LEVELS):
-            slab = slab + slabs[k][lax.rem(level + step, LEVELS)].astype(F32)
-        total[:, :, at : at + width] = slab
+        total[:, :, at : at + width] = scatters[k].result()
+        cols = (slice(None), slice(None), pl.ds(at, width))
+        results.append(
+            pltpu.make_async_copy(total.at[cols], total_out.at[cols], result_sem.at[k])
+        )
+        results[-1].start()
+    for copy in results:
+        copy.wait()
     for copy in near + values + [copy for copies in back for copy in copies]:
         copy.wait_send()
-    for spread in [far, levels, far_values] + gathers + scatters:
+    for spread in [far, levels, far_values] + scatters:
         spread.wait_send()
 
 
@@ -552,9 +675,11 @@
     return pltpu.CompilerParams(vmem_limit_bytes=mebibytes * 2**20, **more)
 
 
-def exchange(mine, offset, own):
-    slab, orbitals = own.shape[0], offset.shape[0] // 3
+def exchange(partner, first, offset, own):
+    slab, orbitals = own.shape[0], offset.shape[1]
     constants = [jnp.asarray(table) for table in tables()]
+    half_slabs = [pltpu.VMEM((2, slab // 2, ORB_DEV, width), BF16) for _, width in CHUNKS]
+    two_slabs = [pltpu.VMEM((2, slab, ORB_DEV, width), BF16) for _, width in CHUNKS]
     boxes = [pltpu.VMEM((SLOTS, EDGE, width), BF16) for _, width in CHUNKS]
     slabs = [pltpu.VMEM((LEVELS, slab, ORB_DEV, width), BF16) for _, width in CHUNKS]
     any_place = pl.BlockSpec(memory_space=pl.ANY)
@@ -565,10 +690,10 @@
             jax.ShapeDtypeStruct((slab, ORB_DEV, AREA), F32),
             jax.ShapeDtypeStruct((orbitals, orbitals), F32),
         ),
-        in_specs=[SMEM, SMEM, VMEM, VMEM, VMEM, any_place, VMEM, VMEM],
-        out_specs=(VMEM,) * 2,
+        in_specs=[SMEM] * 3 + [VMEM] * 4 + [any_place, VMEM, VMEM],
+        out_specs=(any_place,) * 2,
         scratch_shapes=[
-            *slabs, *boxes, *boxes, *boxes, *boxes, *slabs,
+            *slabs, *boxes, *boxes, *boxes, *boxes, *half_slabs, *two_slabs,
             pltpu.VMEM((LEVELS, PEERS, 2, 128), jnp.int32),
             pltpu.VMEM((1, 128), F32),
             pltpu.VMEM((LEVELS, 1, 128), F32),
@@ -583,21 +708,26 @@
             pltpu.VMEM((BATCH * EDGE, PADDED), F32),
             pltpu.VMEM((BATCH * EDGE, 1664), F32),
             pltpu.VMEM((80, AREA), F32),
+            pltpu.VMEM((slab, ORB_DEV, AREA), F32),
+            pltpu.VMEM((orbitals, orbitals), F32),
+            pltpu.VMEM((2, 128), jnp.int32),
             dma((PEERS,)), dma((PEERS,)),
             dma((COUNT, PEERS)), dma((COUNT, PEERS)),
             dma((COUNT, PEERS)), dma((COUNT, PEERS)),
             dma((PEERS,)), dma((PEERS,)),
             dma((2 * COUNT + 3, LEVELS)), dma((2 * COUNT + 3, LEVELS)),
-            dma(()),
+            dma(()), dma((COUNT + 1,)),
         ],
         compiler_params=params(62, collective_id=1, has_side_effects=True),
         name="exchange",
-    )(mine.reshape(-1), offset, mine, own, *constants)
+    )(partner, first, offset, partner, first, own, *constants)
 
 
 def on_device(orbitals, box_offset, partner_slot, first_slot):
-    mine = jnp.concatenate([partner_slot, first_slot], 0).reshape(2, -1)
-    terms, gram = exchange(mine, box_offset.reshape(-1), orbitals.transpose(1, 0, 2))
+    terms, gram = exchange(
+        partner_slot.reshape(1, -1), first_slot.reshape(1, -1), box_offset.T,
+        orbitals.transpose(1, 0, 2),
+    )
     return (terms.transpose(1, 0, 2), gram)
 
 

time: 192 us -> 181 us (0.943)
  the two profiles are of different devices: /device:TPU:86 before, /device:TPU:1 now
where the time goes in v4:
time: 181 us; the launch traced here: 179 us
  Pallas kernels  170 us (94%)
  local copies, waits for them, and re-layouts  8.02 us (4%)
    pallas_call x1, Pallas kernels, exchange(): pl.pallas_call(exchange_kernel, out_shape=(jax.ShapeDtypeStruct((slab, OR...  170 us
    unnamed x6, local copies, waits for them, and re-layouts  6.79 us

profile of v4, /device:TPU:1, one launch (start us, length us, event | category | flops | bytes accessed | tf_op | source)
XLA Modules:
  0.0 179.1 jit_solution(3074298051719625006)
XLA Ops:
  0.6 0.8 copy.12
  1.4 0.6 reshape.10.partner.partner_row
  2.0 0.8 copy.13
  2.8 0.6 reshape.11.first.first_row
  3.4 170.4 %exchange.1 = (f32[10,32,1600]{2,1,0:T(8,128)}, f32[1024,1024]{1,0:T(8,128)}) custom-call(s32[1,128]{1,0:T(1,128)} %reshape.10.partner.partner_row, s32[1,128]{1,0:T(1,128)} %reshape.11.first.first_row, s32[3,1024]{1,0:T(4,128)} %bitcast.5, s32[1,128]{1,0:T(1,128)} %reshape.10.partner.partner_row, s32[1,128]{1,0:T(1,128)} %reshape.11.first.first_row, ...), custom_call_target="tpu_custom_call" | custom-call | tf_op jit(solution)/shard_map/exchange/pallas_call | solution.py:687
  173.8 0.0 copy-start
  173.8 3.2 %copy.16 = f32[32,10,1600]{2,0,1:T(8,128)} copy(f32[32,10,1600]{2,0,1:T(8,128)} %bitcast.3) | data formatting | bytes 4096000
  177.0 0.0 copy-done
  177.1 2.0 %copy.17 = f32[1024,1024]{1,0:T(8,128)} copy(f32[1024,1024]{1,0:T(8,128)S(1)} %copy-done) | data formatting | bytes 8388608
Async XLA Ops:
  173.8 3.3 %copy-start = (f32[1024,1024]{1,0:T(8,128)S(1)}, f32[1024,1024]{1,0:T(8,128)}, u32[]{:S(2)}) copy-start(f32[1024,1024]{1,0:T(8,128)} %get-tuple-element.9) | copy-start | bytes 12582916

commit v5 on v4

--- a/solution.py
+++ b/solution.py
@@ -24,11 +24,11 @@
 STEP = 896
 AHEAD = 2
 LAGS = (0,0,1,2)
-AT_ONCE = (5,5,3,3)
+AT_ONCE = (6,6,3,3)
 TOP = 24
 LEFT = 896
 TILES = [(at, min(128, AREA - at)) for at in range(0, AREA, 128)]
-WIDTHS = (256, 256, 384, 384, 320)
+WIDTHS = (128, 256, 384, 384, 256, 192)
 CHUNKS = [(sum(WIDTHS[:k]), width) for k, width in enumerate(WIDTHS)]
 COUNT = len(CHUNKS)
 PEERS = 8
@@ -348,9 +348,8 @@
 
     def deltas_of(slot):
         at = place_of(slot)
-        partner, first = mine
-        i = me * ORB_DEV + jnp.maximum(first[0, at], 0)
-        j = peer_of(me, level, div(slot, CAP)) * ORB_DEV + jnp.maximum(partner[0, at], 0)
+        i = me * ORB_DEV + jnp.maximum(mine[1, at], 0)
+        j = peer_of(me, level, div(slot, CAP)) * ORB_DEV + jnp.maximum(mine[0, at], 0)
         return tuple(offset[axis, i] - offset[axis, j] for axis in range(3))
 
     def split(value):
@@ -453,8 +452,8 @@
     lax.fori_loop(0, BATCH // 2, after, 0)
 
 
-def add_gram(me, lists, energies, gram, half):
-    orbitals = gram.shape[0]
+def add_gram(me, lists, energies, half, levels):
+    orbitals = half.shape[0]
     row = lax.broadcasted_iota(jnp.int32, (orbitals, 128), 0)
     slot = lax.broadcasted_iota(jnp.int32, (orbitals, 128), 1)
     owner_here = lax.div(row, ORB_DEV) == lax.div(slot, CAP)
@@ -479,7 +478,11 @@
         half[rows, :] = out[0:32] + out[32:64] + out[64:96]
         return 0
 
-    lax.fori_loop(0, LEVELS * PEERS, owner, 0)
+    lax.fori_loop(levels[0] * PEERS, levels[1] * PEERS, owner, 0)
+
+
+def mirror_gram(gram, half):
+    orbitals = gram.shape[0]
     for y in range(0, orbitals, 128):
         for x in range(0, orbitals, 128):
             gram[y : y + 128, x : x + 128] = (
@@ -488,7 +491,7 @@
 
 
 def exchange_kernel(
-    partner, first, offset, partner_row, first_row, own, sine_pair, plane_source, green,
+    listed, offset, mine, own, sine_pair, plane_source, green,
     along_z, total_out, gram_out, *refs,
 ):
     count = COUNT
@@ -499,9 +502,9 @@
     refs = refs[7 * count :]
     lists, energy, column, energies, half, plane = refs[:6]
     scratch = refs[6:14]
-    total, gram, mine = refs[14:17]
-    list_send, list_receive, out_send, out_receive, back_send, back_receive = refs[17:23]
-    value_send, value_receive, level_send, level_receive, plane_sem, result_sem = refs[23:]
+    total, gram = refs[14:16]
+    list_send, list_receive, out_send, out_receive, back_send, back_receive = refs[16:22]
+    value_send, value_receive, level_send, level_receive, plane_sem, result_sem = refs[22:]
     me, level = lax.axis_index("orb"), lax.axis_index("grid")
 
     out, back, near, values = [], [], [], []
@@ -555,8 +558,6 @@
     load_plane = pltpu.make_async_copy(plane_source, plane, plane_sem)
 
     load_plane.start()
-    mine[0:1, :] = partner_row[...]
-    mine[1:2, :] = first_row[...]
     greet(me, level)
     for copy in near:
         copy.start()
@@ -610,7 +611,7 @@
                 out[r][k].wait_recv()
                 out[r][k].wait_send()
         solve_group(
-            me, level, group, (partner, first), offset,
+            me, level, group, listed, offset,
             (partners, phis), (products, own_terms),
             (sine_pair, plane, green, along_z), scratch, energy,
         )
@@ -622,6 +623,7 @@
         gather.wait_send()
     levels.start()
     column[level] = energy[...]
+    results = [pltpu.make_async_copy(gram, gram_out, result_sem.at[count])]
     back_select = jnp.concatenate([asked, ahead], 0).T.astype(BF16)
     levels.wait_recv()
     for copy in values:
@@ -651,11 +653,15 @@
             for copy in values:
                 copy.wait_recv()
             far_values.start()
+        if k == 1:
+            far_values.wait_recv()
+            add_gram(me, lists, energies, half, (0, 2))
+        if k == 2:
+            add_gram(me, lists, energies, half, (2, 4))
+        if k == 3:
+            mirror_gram(gram, half)
+            results[0].start()
     scatters[count - 1].forward()
-    far_values.wait_recv()
-    add_gram(me, lists, energies, gram, half)
-    results = [pltpu.make_async_copy(gram, gram_out, result_sem.at[count])]
-    results[0].start()
     for k, (at, width) in enumerate(CHUNKS):
         total[:, :, at : at + width] = scatters[k].result()
         cols = (slice(None), slice(None), pl.ds(at, width))
@@ -675,7 +681,7 @@
     return pltpu.CompilerParams(vmem_limit_bytes=mebibytes * 2**20, **more)
 
 
-def exchange(partner, first, offset, own):
+def exchange(mine, offset, own):
     slab, orbitals = own.shape[0], offset.shape[1]
     constants = [jnp.asarray(table) for table in tables()]
     half_slabs = [pltpu.VMEM((2, slab // 2, ORB_DEV, width), BF16) for _, width in CHUNKS]
@@ -690,7 +696,7 @@
             jax.ShapeDtypeStruct((slab, ORB_DEV, AREA), F32),
             jax.ShapeDtypeStruct((orbitals, orbitals), F32),
         ),
-        in_specs=[SMEM] * 3 + [VMEM] * 4 + [any_place, VMEM, VMEM],
+        in_specs=[SMEM] * 2 + [VMEM] * 3 + [any_place, VMEM, VMEM],
         out_specs=(any_place,) * 2,
         scratch_shapes=[
             *slabs, *boxes, *boxes, *boxes, *boxes, *half_slabs, *two_slabs,
@@ -710,7 +716,6 @@
             pltpu.VMEM((80, AREA), F32),
             pltpu.VMEM((slab, ORB_DEV, AREA), F32),
             pltpu.VMEM((orbitals, orbitals), F32),
-            pltpu.VMEM((2, 128), jnp.int32),
             dma((PEERS,)), dma((PEERS,)),
             dma((COUNT, PEERS)), dma((COUNT, PEERS)),
             dma((COUNT, PEERS)), dma((COUNT, PEERS)),
@@ -720,12 +725,12 @@
         ],
         compiler_params=params(62, collective_id=1, has_side_effects=True),
         name="exchange",
-    )(partner, first, offset, partner, first, own, *constants)
+    )(mine, offset, mine, own, *constants)
 
 
 def on_device(orbitals, box_offset, partner_slot, first_slot):
     terms, gram = exchange(
-        partner_slot.reshape(1, -1), first_slot.reshape(1, -1), box_offset.T,
+        jnp.concatenate([partner_slot, first_slot], 0).reshape(2, -1), box_offset.T,
         orbitals.transpose(1, 0, 2),
     )
     return (terms.transpose(1, 0, 2), gram)

time: 181 us -> 179 us (0.989); the launches traced: 179 us -> 179 us
  Pallas kernels: 170 us -> 172 us
  local copies, waits for them, and re-layouts: 8.02 us -> 6.03 us
    unnamed x6 -> x4, local copies, waits for them, and re-layouts: 6.79 us -> 5.26 us
where the time goes in v5:
time: 179 us
  Pallas kernels  172 us (96%)
  local copies, waits for them, and re-layouts  6.03 us (3%)
    pallas_call x1, Pallas kernels, exchange(): pl.pallas_call(exchange_kernel, out_shape=(jax.ShapeDtypeStruct((slab, OR...  172 us
    unnamed x4, local copies, waits for them, and re-layouts  5.26 us

profile of v5, /device:TPU:1, one launch (start us, length us, event | category | flops | bytes accessed | tf_op | source)
XLA Modules:
  0.0 179.3 jit_solution(5642372015200218821)
XLA Ops:
  0.6 0.7 pad_add_fusion
  1.3 0.1 copy.11
  1.4 0.7 reshape.7.listed.mine
  2.1 171.9 %exchange.1 = (f32[10,32,1600]{2,1,0:T(8,128)}, f32[1024,1024]{1,0:T(8,128)}) custom-call(s32[2,128]{1,0:T(2,128)} %reshape.7.listed.mine, s32[3,1024]{1,0:T(4,128)} %bitcast.5, s32[2,128]{1,0:T(2,128)} %reshape.7.listed.mine, bf16[10,32,1600]{2,1,0:T(8,128)(2,1)} %bitcast.4, bf16[80,240]{1,0:T(8,128)(2,1)} %constant.8.clone.sine_pair, ...), custom_call_target="tpu_custom_call" | custom-call | tf_op jit(solution)/shard_map/exchange/pallas_call | solution.py:693
  174.0 0.0 copy-start
  174.1 3.2 %copy.14 = f32[32,10,1600]{2,0,1:T(8,128)} copy(f32[32,10,1600]{2,0,1:T(8,128)} %bitcast.3) | data formatting | bytes 4096000
  177.3 0.0 copy-done
  177.3 2.0 %copy.15 = f32[1024,1024]{1,0:T(8,128)} copy(f32[1024,1024]{1,0:T(8,128)S(1)} %copy-done) | data formatting | bytes 8388608
Async XLA Ops:
  174.0 3.3 %copy-start = (f32[1024,1024]{1,0:T(8,128)S(1)}, f32[1024,1024]{1,0:T(8,128)}, u32[]{:S(2)}) copy-start(f32[1024,1024]{1,0:T(8,128)} %get-tuple-element.9) | copy-start | bytes 12582916
